TPU v7x, 256 devices: a whole 4x4x8 slice. The times are simulated.
256 devices in a mesh: gx: 32 (over x, y, core), gy: 8 (over z).
Axes of the slice: x: 4, y: 4, z: 8, core: 2. Of those that a mesh axis runs over, the one named last changes fastest.
Arguments:
- velocity: float32 [4096, 64, 1024], P('gx', None, 'gy'), may hold values from -4.5 to 4.5
- metric: float32 [4096], P('gx'), may hold values from 0.5 to 2
- lower_coupling: float32 [4096], replicated, may hold values from 1024 to 4096
- upper_coupling: float32 [4096], replicated, may hold values from 64 to 256
- cross_diffusion: float32 [1024], P('gy'), may hold values from 0.1 to 0.45
Outputs:
- derivative: float32 [4096, 64, 1024], P('gx', None, 'gy')
- updated: float32 [4096, 64, 1024], P('gx', None, 'gy')
All inputs are finite; a program needn't handle non-finite values.
Results may differ from a plain program's by a relative error of at most 0.00021.
Values sent between devices are 32-bit elements; how exact they have to be, the bound alone decides.
No kernel may reach another device: no remote copies, remote signals or barrier semaphores. Data moves between devices by JAX's collectives and lax.ppermute only.
A program may use at most 128 MiB of HBM per device.

v0:
```python
import functools

import jax
import jax.numpy as jnp
import numpy as np
from jax import lax
from jax.experimental import pallas as pl
from jax.experimental.pallas import tpu as pltpu
from jax.sharding import PartitionSpec as P


ALPHA = 1.0 / 3.0
BODY = 25.0 / 36.0
DIRECT = 1.0 / 12.0
END = 1.0 / 36.0
LANES = 128
CHUNKS = 8
MIB = 1024 * 1024
F32 = jnp.float32
TOKEN = jax.ShapeDtypeStruct((8, LANES), F32)


@functools.lru_cache(maxsize=None)
def slope_constants(blocks, span):
    inner = span - 1
    off = -ALPHA
    fwd = np.ones(span)
    for i in range(1, inner):
        fwd[i] = 1.0 / (1.0 - off * off * fwd[i - 1])
    bwd = np.ones(span)
    for i in range(inner - 2, -1, -1):
        bwd[i] = 1.0 / (1.0 - off * off * bwd[i + 1])
    rho, mu, nu = (fwd.copy(), fwd * off, fwd * off)
    own = np.zeros(span + 2)
    acc = 1.0
    for i in range(inner - 1, -1, -1):
        own[i + 1] = off * rho[i] * acc
        acc *= mu[i]
    through = acc
    own[inner + 1] = 1.0
    first = np.zeros(span + 2)
    acc = 1.0
    for i in range(inner):
        first[i + 1] = bwd[i] * acc
        acc *= bwd[i] * off
    cross = acc
    own_v = np.zeros(span + 2)
    first_v = np.zeros(span + 2)
    for at in range(span + 2):
        low = own[at - 1] if at > 0 else 0.0
        high = own[at + 1] if at < span + 1 else 0.0
        own_v[at] = BODY * (low - high)
        low = first[at - 1] if at > 0 else 0.0
        high = first[at + 1] if at < span + 1 else 0.0
        first_v[at] = BODY * (low - high)
    sum_own = own_v[1 : span + 1].copy()
    sum_next = off * first_v[1 : span + 1]
    sum_next[0] += own_v[span + 1]
    low = off * through
    high = off * cross
    ends = off * bwd[0]
    red = []
    previous = 0.0
    for k in range(blocks):
        middle = 1.0 - off * nu[inner - 1] - (off * ends if k < blocks - 1 else 0.0)
        left = low if k > 0 else 0.0
        right = high if k < blocks - 1 else 0.0
        pivot = 1.0 / (middle - left * previous)
        red.append((pivot, pivot * left, pivot * right))
        previous = pivot * right
    lead = np.zeros(span)
    trail = np.ones(span)
    acc = 1.0
    for i in range(inner):
        acc *= bwd[i] * off
        lead[i] = acc
    acc = 1.0
    for i in range(inner - 1, -1, -1):
        acc *= nu[i]
        trail[i] = acc
    table = [rho * BODY, mu, nu, rho * END, sum_own, sum_next, lead, trail]
    rows = np.stack(table).astype(np.float32)
    weights = {
        "before": float(own_v[0]),
        "after": float(off * first_v[0]),
        "first_end": float(own[1] * END),
        "last_end": float(-own[inner + 1] * END),
    }
    return rows, red, weights


def lane_of(shape):
    return lax.broadcasted_iota(jnp.int32, shape, len(shape) - 1)


def vmem(mib):
    return pltpu.CompilerParams(vmem_limit_bytes=mib * MIB)


def work(ops, reads):
    return pl.CostEstimate(flops=ops, bytes_accessed=reads, transcendentals=0)


def in_vmem(count):
    return [pl.BlockSpec(memory_space=pltpu.VMEM)] * count


def in_hbm(count):
    return [pl.BlockSpec(memory_space=pltpu.HBM)] * count


def in_smem(count):
    return [pl.BlockSpec(memory_space=pltpu.SMEM)] * count


def terms_kernel(
    blocks,
    low_ref,
    up_ref,
    line_ref,
    weight_ref,
    spike_ref,
    row_ref,
    red_ref,
    kap,
    dnow,
    dpre,
    enow,
    enxt,
    factor,
    chain,
    turn,
):
    span = line_ref.shape[1]
    inner = span - 1
    index = lax.axis_index("gx")
    filler = jnp.ones((LANES - blocks, span), F32)
    lower = jnp.transpose(jnp.concatenate([low_ref[...], filler], 0))
    upper = jnp.transpose(jnp.concatenate([up_ref[...], filler], 0))
    row = lax.broadcasted_iota(jnp.int32, (span, LANES), 0)
    lane = lane_of((span, LANES))
    scale = 1.0 / (1.0 + lower + upper)
    alpha = jnp.where((row == 0) & (lane == 0), 0.0, lower * scale)
    gamma = jnp.where((row == inner) & (lane == blocks - 1), 0.0, upper * scale)
    kap[...] = alpha * pltpu.roll(gamma, 1, 0)
    one = jnp.ones((1, LANES), F32)
    dnow[0:1, :] = one
    dpre[0:1, :] = one
    enow[inner - 1 : inner, :] = one
    enxt[inner - 1 : inner, :] = one
    for ref in (dnow, dpre, enow, enxt):
        ref[inner:span, :] = one
    d1, d2, e1, e2 = (one, one, one, one)
    for i in range(1, inner):
        d0 = d1 - kap[i : i + 1, :] * d2
        dpre[i : i + 1, :] = d1
        dnow[i : i + 1, :] = d0
        d2, d1 = (d1, d0)
        j = inner - 1 - i
        e0 = e1 - kap[j + 1 : j + 2, :] * e2
        enxt[j : j + 1, :] = e1
        enow[j : j + 1, :] = e0
        e2, e1 = (e1, e0)
    fwd = dpre[...] / dnow[...]
    bwd = enxt[...] / enow[...]
    rho, mu, nu = (fwd * scale, fwd * alpha, fwd * gamma)
    factor[0] = mu
    factor[1] = bwd * gamma
    factor[2] = bwd * alpha
    factor[3] = nu
    h_acc, g_acc, l_acc, t_acc = (one, one, one, one)
    for i in range(inner):
        j = inner - 1 - i
        chain[0, j : j + 1, :] = h_acc
        chain[1, i : i + 1, :] = g_acc
        h_acc = h_acc * factor[0, j : j + 1, :]
        g_acc = g_acc * factor[1, i : i + 1, :]
        l_acc = l_acc * factor[2, i : i + 1, :]
        t_acc = t_acc * factor[3, j : j + 1, :]
        chain[2, i : i + 1, :] = l_acc
        chain[3, j : j + 1, :] = t_acc
    zero = jnp.zeros((1, LANES), F32)
    chain[0, inner:span, :] = one
    chain[1, inner:span, :] = zero
    chain[2, inner:span, :] = zero
    chain[3, inner:span, :] = one
    alpha_end = alpha[inner:span, :]
    gamma_end = gamma[inner:span, :]
    own = jnp.where(row == inner, 1.0, alpha_end * chain[0]) * rho
    first = bwd * scale * chain[1] * pltpu.roll(gamma_end, 1, 1)
    inflow = bwd[0:1, :] * alpha[0:1, :]
    middle = (
        1.0
        - alpha_end * nu[inner - 1 : inner, :]
        - gamma_end * pltpu.roll(inflow, LANES - 1, 1)
    )
    scale_red = 1.0 / middle
    left = alpha_end * h_acc * scale_red
    right = gamma_end * pltpu.roll(t_acc, LANES - 1, 1) * scale_red
    product = left * pltpu.roll(right, 1, 1)
    for at, value in enumerate((scale_red, left, right, product)):
        turn[at] = jnp.transpose(jnp.broadcast_to(value, (LANES, LANES)))
    d1, d2 = (one, one)
    for k in range(blocks):
        if k == 0:
            ratio = one
        else:
            d0 = d1 - turn[3, k : k + 1, :] * d2
            ratio = d1 / d0
            d2, d1 = (d1, d0)
        for at in range(3):
            red_ref[at, k : k + 1, :] = turn[at, k : k + 1, :] * ratio

    def mine(value):
        column = jnp.sum(jnp.where(lane == index, value, 0.0), axis=1, keepdims=True)
        return jnp.broadcast_to(column, (span, LANES))

    line_ref[0] = mine(rho)
    line_ref[1] = mine(mu)
    line_ref[2] = mine(nu)
    spike_ref[0] = mine(chain[2])
    spike_ref[1] = mine(chain[3])
    for at, value in enumerate((own, first)):
        here = mine(value)
        weight_ref[at] = here
        row_ref[at] = jnp.transpose(here)[0:8, :]


def viscous_terms(lower, upper):
    blocks, span = lower.shape
    square = pltpu.VMEM((span, LANES), F32)
    four = pltpu.VMEM((4, span, LANES), F32)
    return pl.pallas_call(
        functools.partial(terms_kernel, blocks),
        out_shape=(
            jax.ShapeDtypeStruct((3, span, LANES), F32),
            jax.ShapeDtypeStruct((2, span, LANES), F32),
            jax.ShapeDtypeStruct((2, span, LANES), F32),
            jax.ShapeDtypeStruct((2, 8, span), F32),
            jax.ShapeDtypeStruct((3, blocks, LANES), F32),
        ),
        in_specs=in_vmem(2),
        out_specs=tuple(in_vmem(5)),
        scratch_shapes=[square] * 5 + [four, four, pltpu.VMEM((4, LANES, LANES), F32)],
        compiler_params=vmem(8),
        cost_estimate=work(4 * 1024 * 1024, 1024 * 1024),
        name="viscous_terms",
    )(lower, upper)


def chunk_copy(source, target, sem, c):
    rows = source.shape[0] // CHUNKS
    where = pl.ds(c * rows, rows)
    return pltpu.make_async_copy(source.at[where], target.at[where], sem.at[c])


def start_all(source, target, sem):
    for c in range(CHUNKS):
        chunk_copy(source, target, sem, c).start()


def streamed(shape, count):
    return [pltpu.VMEM(shape, F32)] * count


def rim_kernel(v_hbm, first_ref, last_ref, v_buf, sem):
    span, planes, width = v_buf.shape
    rows = span // CHUNKS
    start_all(v_hbm, v_buf, sem)
    lane = lane_of((planes, width))
    zero = jnp.zeros((planes, width), F32)

    def step(c, carry):
        first, last = carry
        chunk_copy(v_hbm, v_buf, sem, c).wait()
        for r in range(rows):
            i = c * rows + r
            turned = pltpu.roll(v_buf[i], i, 1)
            first = jnp.where(lane == i, turned, first)
            last = jnp.where(lane == lax.rem(i + width - 1, width), turned, last)
        return (first, last)

    first, last = lax.fori_loop(0, CHUNKS, step, (zero, zero))
    first_ref[...] = first
    last_ref[...] = pltpu.roll(last, 1, 1)


def rim_columns(velocity):
    span, planes, width = velocity.shape
    column = jax.ShapeDtypeStruct((planes, width), F32)
    return pl.pallas_call(
        rim_kernel,
        out_shape=(column, column),
        in_specs=in_hbm(1),
        out_specs=tuple(in_vmem(2)),
        scratch_shapes=streamed(velocity.shape, 1) + [pltpu.SemaphoreType.DMA((CHUNKS,))],
        compiler_params=vmem(8),
        name="rim_columns",
    )(velocity)


def sums_kernel(table, v_hbm, weight, vec_ref, v_buf, sem):
    span, planes, width = v_buf.shape
    rows = span // CHUNKS
    start_all(v_hbm, v_buf, sem)
    zero = jnp.zeros((planes, width), F32)

    def step(c, carry):
        a, b, s, t = carry
        chunk_copy(v_hbm, v_buf, sem, c).wait()
        for r in range(rows):
            i = c * rows + r
            v = v_buf[i]
            a = a + weight[0, pl.ds(i, 1), :] * v
            b = b + weight[1, pl.ds(i, 1), :] * v
            s = s + table[4, i] * v
            t = t + table[5, i] * v
        return (a, b, s, t)

    sums = lax.fori_loop(0, CHUNKS, step, (zero, zero, zero, zero))
    for at in range(4):
        vec_ref[at] = sums[at]
    vec_ref[4] = v_buf[0]
    vec_ref[5] = v_buf[span - 1]


def local_sums(table, velocity, weight):
    span, planes, width = velocity.shape
    return pl.pallas_call(
        sums_kernel,
        out_shape=jax.ShapeDtypeStruct((6, planes, width), F32),
        in_specs=in_smem(1) + in_hbm(1) + in_vmem(1),
        out_specs=in_vmem(1)[0],
        scratch_shapes=streamed(velocity.shape, 1) + [pltpu.SemaphoreType.DMA((CHUNKS,))],
        compiler_params=vmem(8),
        cost_estimate=work(8 * velocity.size, 4 * velocity.size),
        name="local_sums",
    )(table, velocity, weight)


def slope_kernel(table, metric, v_hbm, order, out_hbm, v_ref, der, v_sem, out_sem):
    span, planes, width = v_ref.shape
    inner = span - 1
    rows = span // CHUNKS
    start_all(v_hbm, v_ref, v_sem)
    zero = jnp.zeros((planes, width), F32)
    top = jnp.where(lax.axis_index("gx") == 0, 1.0, 0.0).astype(F32)

    def forward(i, carry):
        v_low, v, slo = carry
        v_high = v_ref[i + 1]
        slo = table[0, i] * (v_high - v_low) + table[1, i] * slo
        if isinstance(i, int) and i == 0:
            slo = slo + (table[3, 0] * top) * v
        der[i] = slo
        return (v, v_high, slo)

    def down(c, carry):
        chunk_copy(v_hbm, v_ref, v_sem, c + 1).wait()
        for r in range(rows):
            carry = forward(c * rows + r, carry)
        return carry

    chunk_copy(v_hbm, v_ref, v_sem, 0).wait()
    carry = down(0, (zero, v_ref[0], zero))
    carry = lax.fori_loop(1, CHUNKS - 1, down, carry)
    for i in range(span - rows, inner):
        carry = forward(i, carry)

    def finish(i, slo, difference):
        scale = metric[i]
        return scale * slo + (scale * DIRECT) * difference

    def backward(i, slo, difference):
        slo = der[i] + table[2, i] * slo
        der[i] = finish(i, slo, difference)
        return slo

    def up(step, slo):
        c = CHUNKS - 1 - step
        for r in range(rows - 1, -1, -1):
            i = c * rows + r
            slo = backward(i, slo, v_ref[i + 1] - v_ref[i - 1])
        chunk_copy(der, out_hbm, out_sem, c).start()
        return slo

    der[inner] = finish(inner, zero, -v_ref[inner - 1])
    slo = zero
    for i in range(inner - 1, span - 1 - rows, -1):
        slo = backward(i, slo, v_ref[i + 1] - v_ref[i - 1])
    chunk_copy(der, out_hbm, out_sem, CHUNKS - 1).start()
    slo = lax.fori_loop(1, CHUNKS - 1, up, slo)
    for i in range(rows - 1, -1, -1):
        slo = backward(i, slo, v_ref[i + 1] - v_ref[i - 1] if i else v_ref[1])
    chunk_copy(der, out_hbm, out_sem, 0).start()
    for c in range(CHUNKS):
        chunk_copy(der, out_hbm, out_sem, c).wait()


def slope_solve(table, metric, velocity, order):
    return pl.pallas_call(
        slope_kernel,
        out_shape=pltpu.HBM(velocity.shape, F32),
        in_specs=in_smem(2) + in_hbm(1) + [pl.BlockSpec(memory_space=pl.ANY)],
        out_specs=in_hbm(1)[0],
        scratch_shapes=streamed(velocity.shape, 2) + [pltpu.SemaphoreType.DMA((CHUNKS,))] * 2,
        compiler_params=vmem(12),
        cost_estimate=work(12 * velocity.size, 12 * velocity.size),
        name="slope_solve",
    )(table, metric, velocity, order)


def viscous_kernel(
    v_hbm,
    line,
    before_ref,
    after_ref,
    cross_ref,
    order,
    out_hbm,
    v_ref,
    upd,
    even,
    odd,
    v_sem,
    out_sem,
):
    span, planes, width = v_ref.shape
    inner = span - 1
    rows = span // CHUNKS
    start_all(v_hbm, v_ref, v_sem)
    lane = lane_of((planes, width))
    ahead = pltpu.roll(after_ref[...], width - 1, 1)
    even[...] = jnp.where(lax.rem(lane, 2) == 0, before_ref[...], ahead)
    odd[...] = jnp.where(lax.rem(lane, 2) == 1, before_ref[...], ahead)
    cross = jnp.broadcast_to(cross_ref[...], (planes, width))
    keep = 1.0 - 2.0 * cross
    zero = jnp.zeros((planes, width), F32)

    def forward(i, r, vis):
        v = v_ref[i]
        rim = pltpu.roll((odd if r % 2 else even)[...], lax.rem(width - i, width), 1)
        low = jnp.where(lane == 0, rim, pltpu.roll(v, 1, 1))
        high = jnp.where(lane == width - 1, rim, pltpu.roll(v, width - 1, 1))
        rhs = keep * v + cross * (low + high)
        vis = line[0, pl.ds(i, 1), :] * rhs + line[1, pl.ds(i, 1), :] * vis
        upd[i] = vis
        return vis

    def down(c, vis):
        chunk_copy(v_hbm, v_ref, v_sem, c).wait()
        for r in range(rows):
            vis = forward(c * rows + r, r, vis)
        return vis

    lax.fori_loop(0, CHUNKS, down, zero)

    def backward(i, vis):
        vis = upd[i] + line[2, pl.ds(i, 1), :] * vis
        upd[i] = vis
        return vis

    def up(step, vis):
        c = CHUNKS - 1 - step
        for r in range(rows - 1, -1, -1):
            vis = backward(c * rows + r, vis)
        chunk_copy(upd, out_hbm, out_sem, c).start()
        return vis

    upd[inner] = zero
    vis = zero
    for i in range(inner - 1, span - 1 - rows, -1):
        vis = backward(i, vis)
    chunk_copy(upd, out_hbm, out_sem, CHUNKS - 1).start()
    lax.fori_loop(1, CHUNKS, up, vis)
    for c in range(CHUNKS):
        chunk_copy(upd, out_hbm, out_sem, c).wait()


def viscous_solve(velocity, line, before, after, cross, order):
    span, planes, width = velocity.shape
    return pl.pallas_call(
        viscous_kernel,
        out_shape=pltpu.HBM(velocity.shape, F32),
        in_specs=in_hbm(1) + in_vmem(4) + [pl.BlockSpec(memory_space=pl.ANY)],
        out_specs=in_hbm(1)[0],
        scratch_shapes=streamed(velocity.shape, 2)
        + [pltpu.VMEM((planes, width), F32)] * 2
        + [pltpu.SemaphoreType.DMA((CHUNKS,))] * 2,
        compiler_params=vmem(12),
        cost_estimate=work(12 * velocity.size, 12 * velocity.size),
        name="viscous_solve",
    )(velocity, line, before, after, cross, order)


def wall_normal(value, before, after, cross):
    shape = value.shape
    lane = lane_of(shape)
    low = jnp.where(lane == 0, before, pltpu.roll(value, 1, 1))
    high = jnp.where(lane == shape[1] - 1, after, pltpu.roll(value, shape[1] - 1, 1))
    return (1.0 - 2.0 * cross) * value + cross * (low + high)


def pack_kernel(vec_ref, row_ref, before_ref, after_ref, cross_ref, out_ref, token):
    blocks = out_ref.shape[0]
    part = vec_ref.shape[1] // blocks
    cross = cross_ref[...]
    vectors = []
    for at in range(2):
        weights = row_ref[at, 0:1, :]
        before = jnp.sum(before_ref[...] * weights, axis=1, keepdims=True)
        after = jnp.sum(after_ref[...] * weights, axis=1, keepdims=True)
        vectors.append(wall_normal(vec_ref[at], before, after, cross))
    vectors += [vec_ref[at] for at in range(2, 6)]
    for at, value in enumerate(vectors):
        for m in range(blocks):
            out_ref[m, part * at : part * (at + 1), :] = value[part * m : part * (m + 1), :]
    rest = out_ref.shape[1] - 6 * part
    if rest:
        out_ref[:, 6 * part :, :] = jnp.zeros((blocks, rest, out_ref.shape[2]), F32)
    token[...] = jnp.zeros(token.shape, F32)


def rows_sent(part):
    return -(-6 * part // 8) * 8


def pack(vec, row, before, after, cross, blocks):
    _, planes, width = vec.shape
    part = planes // blocks
    return pl.pallas_call(
        pack_kernel,
        out_shape=(jax.ShapeDtypeStruct((blocks, rows_sent(part), width), F32), TOKEN),
        compiler_params=vmem(8),
        name="pack_sums",
    )(vec, row, before, after, cross)


def reduced_kernel(part, red, weights, coef_ref, in_ref, order, out_ref, token):
    blocks, rows, width = in_ref.shape
    slope_after, slope_before = (weights["after"], weights["before"])

    def piece(k, at):
        return in_ref[k, part * at : part * (at + 1), :]

    zero = jnp.zeros((part, width), F32)
    vis, slo = (zero, zero)
    vis_all, slo_all = ([], [])
    for k in range(blocks):
        vis_rhs = piece(k, 0)
        slo_rhs = piece(k, 2)
        if k < blocks - 1:
            vis_rhs = vis_rhs + piece(k + 1, 1)
            slo_rhs = slo_rhs + piece(k + 1, 3) + slope_after * piece(k, 5)
        else:
            slo_rhs = slo_rhs + weights["last_end"] * piece(k, 5)
        if k > 0:
            slo_rhs = slo_rhs + slope_before * piece(k - 1, 5)
        else:
            slo_rhs = slo_rhs + weights["first_end"] * piece(k, 4)
        vis = coef_ref[0, k : k + 1, :] * vis_rhs + coef_ref[1, k : k + 1, :] * vis
        slo = red[k][0] * slo_rhs + red[k][1] * slo
        vis_all.append(vis)
        slo_all.append(slo)
    vis, slo = (zero, zero)
    rest = rows - 6 * part
    for k in range(blocks - 1, -1, -1):
        vis = vis_all[k] + coef_ref[2, k : k + 1, :] * vis
        slo = slo_all[k] + red[k][2] * slo
        out_ref[k, part : 2 * part, :] = vis
        out_ref[k, 3 * part : 4 * part, :] = slo
        if k < blocks - 1:
            out_ref[k + 1, 0:part, :] = vis
            out_ref[k + 1, 2 * part : 3 * part, :] = slo + (BODY / ALPHA) * piece(k, 5)
        else:
            out_ref[0, 0:part, :] = zero
            out_ref[0, 2 * part : 3 * part, :] = zero
        out_ref[k, 4 * part : 5 * part, :] = piece(k - 1, 5) if k > 0 else zero
        out_ref[k, 5 * part : 6 * part, :] = piece(k + 1, 4) if k < blocks - 1 else zero
    if rest:
        out_ref[:, 6 * part :, :] = jnp.zeros((blocks, rest, width), F32)
    token[...] = jnp.zeros(token.shape, F32)


def reduced_solve(coef, arrived, order, red, weights, part):
    return pl.pallas_call(
        functools.partial(reduced_kernel, part, red, weights),
        out_shape=(jax.ShapeDtypeStruct(arrived.shape, F32), TOKEN),
        in_specs=in_vmem(2) + in_hbm(1),
        out_specs=tuple(in_vmem(2)),
        compiler_params=vmem(8),
        name="reduced_solve",
    )(coef, arrived, order)


def final_kernel(
    table,
    metric,
    der_in,
    upd_in,
    edge_ref,
    spike,
    der_hbm,
    upd_hbm,
    der,
    upd,
    edges,
    der_from,
    upd_from,
    der_to,
    upd_to,
):
    span, planes, width = der.shape
    blocks = edge_ref.shape[0]
    part = planes // blocks
    rows = span // CHUNKS
    for c in range(CHUNKS):
        chunk_copy(der_in, der, der_from, c).start()
        chunk_copy(upd_in, upd, upd_from, c).start()
    for at in range(6):
        for m in range(blocks):
            edges[at, part * m : part * (m + 1), :] = edge_ref[m, part * at : part * (at + 1), :]
    vis_low, vis_high, slo_low, slo_high = (edges[at] for at in range(4))

    def step(c, carry):
        chunk_copy(der_in, der, der_from, c).wait()
        chunk_copy(upd_in, upd, upd_from, c).wait()
        for r in range(rows):
            i = c * rows + r
            scale = metric[i]
            der[i] = der[i] + (scale * table[6, i]) * slo_low + (scale * table[7, i]) * slo_high
            upd[i] = (
                upd[i] + spike[0, pl.ds(i, 1), :] * vis_low + spike[1, pl.ds(i, 1), :] * vis_high
            )
        if isinstance(c, int) and c == 0:
            der[0] = der[0] - (metric[0] * DIRECT) * edges[4]
        if isinstance(c, int) and c == CHUNKS - 1:
            der[span - 1] = der[span - 1] + (metric[span - 1] * DIRECT) * edges[5]
        chunk_copy(der, der_hbm, der_to, c).start(priority=1)
        chunk_copy(upd, upd_hbm, upd_to, c).start(priority=1)
        return carry

    step(0, 0)
    lax.fori_loop(1, CHUNKS - 1, step, 0)
    step(CHUNKS - 1, 0)
    for c in range(CHUNKS):
        chunk_copy(der, der_hbm, der_to, c).wait()
        chunk_copy(upd, upd_hbm, upd_to, c).wait()


def final_solve(table, metric, der, upd, edge, spike):
    span, planes, width = der.shape
    result = jax.ShapeDtypeStruct(der.shape, F32)
    return pl.pallas_call(
        final_kernel,
        out_shape=(result, result),
        in_specs=in_smem(2) + in_hbm(2) + in_vmem(2),
        out_specs=tuple(in_hbm(2)),
        scratch_shapes=streamed(der.shape, 2)
        + [pltpu.VMEM((6, planes, width), F32)]
        + [pltpu.SemaphoreType.DMA((CHUNKS,))] * 4,
        compiler_params=vmem(16),
        name="final_solve",
    )(table, metric, der, upd, edge, spike)


def body(velocity, metric, lower_coupling, upper_coupling, cross_diffusion):
    span, planes, width = velocity.shape
    blocks = lax.axis_size("gx")
    walls = lax.axis_size("gy")
    part = planes // blocks
    rows, red, weights = slope_constants(blocks, span)
    table = jnp.asarray(rows)
    cross = cross_diffusion.reshape(1, width)
    line, weight, spike, row, coef = viscous_terms(
        lower_coupling.reshape(blocks, span), upper_coupling.reshape(blocks, span)
    )
    field = pltpu.with_memory_space_constraint(velocity, pltpu.HBM)
    first, last = rim_columns(field)
    up = [(j, j + 1) for j in range(walls - 1)]
    down = [(j + 1, j) for j in range(walls - 1)]
    before = lax.ppermute(last, "gy", up)
    after = lax.ppermute(first, "gy", down)
    vec = local_sums(table, field, weight)
    packed, token = pack(vec, row, before, after, cross, blocks)
    arrived = lax.all_to_all(packed, "gx", 0, 0, tiled=True)
    der = slope_solve(table, metric, field, token)
    der = pltpu.with_memory_space_constraint(der, pltpu.HBM)
    solved, token = reduced_solve(coef, arrived, der, red, weights, part)
    edge = lax.all_to_all(solved, "gx", 0, 0, tiled=True)
    upd = viscous_solve(field, line, before, after, cross, token)
    upd = pltpu.with_memory_space_constraint(upd, pltpu.HBM)
    return final_solve(table, metric, der, upd, edge, spike)


def solution(mesh):
    return jax.shard_map(
        body,
        mesh=mesh,
        in_specs=(P("gx", None, "gy"), P("gx"), P(), P(), P("gy")),
        out_specs=(P("gx", None, "gy"), P("gx", None, "gy")),
        check_vma=False,
    )
```

profile of v0, /device:TPU:97, one launch (start us, length us, event | category | flops | bytes accessed | tf_op | source)
XLA Modules:
  0.0 54.5 jit_solution(9941088994831174001)
XLA Ops:
  0.6 0.0 copy-start
  0.6 0.0 copy-start.2
  0.7 0.0 copy-start.1
  0.7 0.0 copy-start.3
  0.7 0.0 copy-start.4
  0.7 2.8 %rim_columns.1 = (f32[64,128]{1,0:T(8,128)S(1)}, f32[64,128]{1,0:T(8,128)S(1)}) custom-call(f32[128,64,128]{2,1,0:T(8,128)} %v_hbm.7), custom_call_target="tpu_custom_call" | custom-call | tf_op jit(solution)/shard_map/rim_columns/pallas_call | solution.py:291
  3.5 4.8 %collective-permute-start = (f32[64,128]{1,0:T(8,128)S(1)}, f32[64,128]{1,0:T(8,128)S(1)}, u32[]{:S(2)}, u32[]{:S(2)}) collective-permute-start(f32[64,128]{1,0:T(8,128)S(1)} %get-tuple-element.15), channel_id=1, source_target_pairs={{0,1},{1,2},{2,3},{3,4},{4,5},{5,6},{6,7},{8,9},{9,10},{10,11},{11... | collective-permute-start | bytes 98312 | tf_op jit(solution)/shard_map/ppermute | solution.py:682
  8.3 1.9 %collective-permute-start.1 = (f32[64,128]{1,0:T(8,128)S(1)}, f32[64,128]{1,0:T(8,128)S(1)}, u32[]{:S(2)}, u32[]{:S(2)}) collective-permute-start(f32[64,128]{1,0:T(8,128)S(1)} %get-tuple-element.16), channel_id=1, source_target_pairs={{1,0},{2,1},{3,2},{4,3},{5,4},{6,5},{7,6},{9,8},{10,9},{11,10},{12... | collective-permute-start | bytes 98312 | tf_op jit(solution)/shard_map/ppermute | solution.py:683
  10.2 0.0 copy-done.2
  10.2 0.0 copy-done.1
  10.2 0.9 %viscous_terms.1 = (f32[3,128,128]{2,1,0:T(8,128)S(1)}, f32[2,128,128]{2,1,0:T(8,128)S(1)}, f32[2,128,128]{2,1,0:T(8,128)S(1)}, f32[2,8,128]{2,1,0:T(8,128)S(1)}, f32[3,32,128]{2,1,0:T(8,128)S(1)}) custom-call(f32[32,128]{1,0:T(8,128)S(1)} %bitcast.3, f32[32,128]{1,0:T(8,128)S(1)} %bitcast.4), custom_call_target="tpu_custom_call" | custom-call | flops 4194304 | bytes 1048576 | tf_op jit(solution)/shard_map/viscous_terms/pallas_call | solution.py:233
  11.2 0.0 copy-done
  11.2 3.0 %local_sums.1.vec_ref = f32[6,64,128]{2,1,0:T(8,128)S(1)} custom-call(f32[8,128]{1,0:T(8,128)S(1)} %copy-done, f32[128,64,128]{2,1,0:T(8,128)} %v_hbm.7, f32[2,128,128]{2,1,0:T(8,128)S(1)} %get-tuple-element.13.weight), custom_call_target="tpu_custom_call" | custom-call | flops 8388608 | bytes 4194304 | tf_op jit(solution)/shard_map/local_sums/pallas_call | solution.py:329
  14.1 0.0 collective-permute-done.before_ref
  14.2 0.0 collective-permute-done.1.after_ref
  14.2 0.9 %pack_sums.1 = (f32[32,16,128]{2,1,0:T(8,128)}, f32[8,128]{1,0:T(8,128)S(1)}) custom-call(f32[6,64,128]{2,1,0:T(8,128)S(1)} %local_sums.1.vec_ref, f32[2,8,128]{2,1,0:T(8,128)S(1)} %get-tuple-element.14.row_ref, f32[64,128]{1,0:T(8,128)S(1)} %collective-permute-done.before_ref, f32[64,128]{1,0:T(8,128)S(1)} %collective-permute-done.1.after_ref, ...), custom_call_target="tpu_custom_call" | custom-call | tf_op jit(solution)/shard_map/pack_sums/pallas_call | solution.py:531
  15.1 9.2 %all-to-all-start = ((f32[32,16,128]{2,1,0:T(8,128)}), f32[32,16,128]{2,1,0:T(8,128)S(1)}, u32[]{:S(2)}, u32[]{:S(2)}) async-start(f32[32,16,128]{2,1,0:T(8,128)} %get-tuple-element.20), calls=%async_computation | async-start | bytes 524288 | tf_op jit(solution)/shard_map/all_to_all | solution.py:686
  24.3 5.1 %slope_solve.1.order.der_in = f32[128,64,128]{2,1,0:T(8,128)} custom-call(f32[8,128]{1,0:T(8,128)S(1)} %copy-done, f32[128]{0:T(128)S(1)} %copy-done.4, f32[128,64,128]{2,1,0:T(8,128)} %v_hbm.7, f32[8,128]{1,0:T(8,128)S(1)} %get-tuple-element.17.order), custom_call_target="tpu_custom_call" | custom-call | flops 12582912 | bytes 12582912 | tf_op jit(solution)/shard_map/slope_solve/pallas_call | solution.py:401
  29.4 3.8 %all-to-all-done.in_ref = f32[32,16,128]{2,1,0:T(8,128)S(1)} async-done(((f32[32,16,128]{2,1,0:T(8,128)}), f32[32,16,128]{2,1,0:T(8,128)S(1)}, u32[]{:S(2)}, u32[]{:S(2)}) %all-to-all-start) | async-done | bytes 262176 | tf_op jit(solution)/shard_map/all_to_all | solution.py:686
  33.2 0.9 %reduced_solve.1 = (f32[32,16,128]{2,1,0:T(8,128)}, f32[8,128]{1,0:T(8,128)S(1)}) custom-call(f32[3,32,128]{2,1,0:T(8,128)S(1)} %get-tuple-element.19.coef_ref, f32[32,16,128]{2,1,0:T(8,128)S(1)} %all-to-all-done.in_ref, f32[128,64,128]{2,1,0:T(8,128)} %slope_solve.1.order.der_in), custom_call_target="tpu_custom_call" | custom-call | tf_op jit(solution)/shard_map/reduced_solve/pallas_call | solution.py:586
  34.1 3.7 %all-to-all-start.1 = ((f32[32,16,128]{2,1,0:T(8,128)}), f32[32,16,128]{2,1,0:T(8,128)S(1)}, u32[]{:S(2)}, u32[]{:S(2)}) async-start(f32[32,16,128]{2,1,0:T(8,128)} %get-tuple-element.22), calls=%async_computation.1 | async-start | bytes 524288 | tf_op jit(solution)/shard_map/all_to_all | solution.py:690
  37.8 7.0 %viscous_solve.1.upd_in = f32[128,64,128]{2,1,0:T(8,128)} custom-call(f32[128,64,128]{2,1,0:T(8,128)} %v_hbm.7, f32[3,128,128]{2,1,0:T(8,128)S(1)} %get-tuple-element.18.line, f32[64,128]{1,0:T(8,128)S(1)} %collective-permute-done.before_ref, f32[64,128]{1,0:T(8,128)S(1)} %collective-permute-done.1.after_ref, f32[1,128]{1,0:T(1,128)S(1)} %bitcast.6, ...), custom_call_target="tpu_custom_call" | custom-call | flops 12582912 | bytes 12582912 | tf_op jit(solution)/shard_map/viscous_solve/pallas_call | solution.py:482
  44.9 2.0 %all-to-all-done.1.edge_ref = f32[32,16,128]{2,1,0:T(8,128)S(1)} async-done(((f32[32,16,128]{2,1,0:T(8,128)}), f32[32,16,128]{2,1,0:T(8,128)S(1)}, u32[]{:S(2)}, u32[]{:S(2)}) %all-to-all-start.1) | async-done | bytes 262176 | tf_op jit(solution)/shard_map/all_to_all | solution.py:690
  46.9 7.6 %final_solve.1 = (f32[128,64,128]{2,1,0:T(8,128)}, f32[128,64,128]{2,1,0:T(8,128)}) custom-call(f32[8,128]{1,0:T(8,128)S(1)} %copy-done, f32[128]{0:T(128)S(1)} %copy-done.4, f32[128,64,128]{2,1,0:T(8,128)} %slope_solve.1.order.der_in, f32[128,64,128]{2,1,0:T(8,128)} %viscous_solve.1.upd_in, f32[32,16,128]{2,1,0:T(8,128)S(1)} %all-to-all-done.1.edge_ref, ...), custom_call_target="tpu_custom_call" | custom-call | tf_op jit(solution)/shard_map/final_solve/pallas_call | solution.py:654
  (2 shorter events, 0.0 us)
Async XLA Ops:
  0.6 10.5 %copy-start = (f32[8,128]{1,0:T(8,128)S(1)}, f32[8,128]{1,0:T(8,128)}, u32[]{:S(2)}) copy-start(f32[8,128]{1,0:T(8,128)} %constant.2.clone.table) | copy-start | bytes 12292
  0.6 9.6 %copy-start.2 = (f32[4096]{0:T(1024)S(1)}, f32[4096]{0:T(1024)}, u32[]{:S(2)}) copy-start(f32[4096]{0:T(1024)} %param.9) | copy-start | bytes 49156
  0.7 9.6 %copy-start.1 = (f32[4096]{0:T(1024)S(1)}, f32[4096]{0:T(1024)}, u32[]{:S(2)}) copy-start(f32[4096]{0:T(1024)} %param.8) | copy-start | bytes 49156
  0.7 13.5 %copy-start.3 = (f32[128]{0:T(128)S(1)}, f32[128]{0:T(128)}, u32[]{:S(2)}) copy-start(f32[128]{0:T(128)} %param.10) | copy-start | bytes 1540
  0.7 23.6 %copy-start.4 = (f32[128]{0:T(128)S(1)}, f32[128]{0:T(128)}, u32[]{:S(2)}) copy-start(f32[128]{0:T(128)} %metric.3) | copy-start | bytes 1540
  3.5 10.6 %collective-permute-start = (f32[64,128]{1,0:T(8,128)S(1)}, f32[64,128]{1,0:T(8,128)S(1)}, u32[]{:S(2)}, u32[]{:S(2)}) collective-permute-start(f32[64,128]{1,0:T(8,128)S(1)} %get-tuple-element.15), channel_id=1, source_target_pairs={{0,1},{1,2},{2,3},{3,4},{4,5},{5,6},{6,7},{8,9},{9,10},{10,11},{11... | collective-permute-start | bytes 98312 | tf_op jit(solution)/shard_map/ppermute | solution.py:682
  8.3 5.9 %collective-permute-start.1 = (f32[64,128]{1,0:T(8,128)S(1)}, f32[64,128]{1,0:T(8,128)S(1)}, u32[]{:S(2)}, u32[]{:S(2)}) collective-permute-start(f32[64,128]{1,0:T(8,128)S(1)} %get-tuple-element.16), channel_id=1, source_target_pairs={{1,0},{2,1},{3,2},{4,3},{5,4},{6,5},{7,6},{9,8},{10,9},{11,10},{12... | collective-permute-start | bytes 98312 | tf_op jit(solution)/shard_map/ppermute | solution.py:683
  15.1 18.2 %all-to-all-start = ((f32[32,16,128]{2,1,0:T(8,128)}), f32[32,16,128]{2,1,0:T(8,128)S(1)}, u32[]{:S(2)}, u32[]{:S(2)}) async-start(f32[32,16,128]{2,1,0:T(8,128)} %get-tuple-element.20), calls=%async_computation | async-start | bytes 524288 | tf_op jit(solution)/shard_map/all_to_all | solution.py:686
  34.1 12.8 %all-to-all-start.1 = ((f32[32,16,128]{2,1,0:T(8,128)}), f32[32,16,128]{2,1,0:T(8,128)S(1)}, u32[]{:S(2)}, u32[]{:S(2)}) async-start(f32[32,16,128]{2,1,0:T(8,128)} %get-tuple-element.22), calls=%async_computation.1 | async-start | bytes 524288 | tf_op jit(solution)/shard_map/all_to_all | solution.py:690
where the time goes:
time: 54.9 us; the launch traced here: 54.5 us
  Pallas kernels  28.3 us (52%)
  starting transfers between devices  19.6 us (36%)
  waiting for transfers between devices  5.9 us (11%)
  between operations  0.78 us (1%)
    all_to_all x1, starting transfers between devices, body(): arrived = lax.all_to_all(packed, 'gx', 0, 0, tiled=True)  9.18 us
    pallas_call x1, Pallas kernels, final_solve(): pl.pallas_call(final_kernel, out_shape=(result, result), in_specs=in_smem...  7.6 us
    pallas_call x1, Pallas kernels, viscous_solve(): pl.pallas_call(viscous_kernel, out_shape=pltpu.HBM(velocity.shape, F32),...  7.05 us
    pallas_call x1, Pallas kernels, slope_solve(): pl.pallas_call(slope_kernel, out_shape=pltpu.HBM(velocity.shape, F32), in...  5.13 us
    ppermute x1, starting transfers between devices, body(): before = lax.ppermute(last, 'gy', up)  4.76 us
    all_to_all x1, waiting for transfers between devices, body(): arrived = lax.all_to_all(packed, 'gx', 0, 0, tiled=True)  3.84 us
    all_to_all x1, starting transfers between devices, body(): edge = lax.all_to_all(solved, 'gx', 0, 0, tiled=True)  3.71 us
    pallas_call x1, Pallas kernels, local_sums(): pl.pallas_call(sums_kernel, out_shape=jax.ShapeDtypeStruct((6, planes, wi...  2.97 us
  transfers between devices with their start and end apart: 4, of which 2 were waited for; matrix products, arithmetic and copies ran while one was open for 0% of the time, Pallas kernels for 29%

commit v1 on v0

--- a/solution.py
+++ b/solution.py
@@ -15,6 +15,7 @@
 END = 1.0 / 36.0
 LANES = 128
 CHUNKS = 8
+KEPT = 5
 MIB = 1024 * 1024
 F32 = jnp.float32
 TOKEN = jax.ShapeDtypeStruct((8, LANES), F32)
@@ -113,7 +114,7 @@
     return [pl.BlockSpec(memory_space=pltpu.SMEM)] * count
 
 
-def terms_kernel(
+def viscous_terms(
     blocks,
     low_ref,
     up_ref,
@@ -226,12 +227,32 @@
         row_ref[at] = jnp.transpose(here)[0:8, :]
 
 
-def viscous_terms(lower, upper):
+def chunk_copy(source, target, sem, c):
+    rows = source.shape[0] // CHUNKS
+    where = pl.ds(c * rows, rows)
+    return pltpu.make_async_copy(source.at[where], target.at[where], sem.at[c])
+
+
+def row_copy(source, target, sem, c, rows):
+    where = pl.ds(c * rows, rows)
+    return pltpu.make_async_copy(source.at[where], target.at[where], sem.at[c])
+
+
+def start_all(source, target, sem):
+    for c in range(CHUNKS):
+        chunk_copy(source, target, sem, c).start()
+
+
+def streamed(shape, count):
+    return [pltpu.VMEM(shape, F32)] * count
+
+
+def block_terms(lower, upper):
     blocks, span = lower.shape
     square = pltpu.VMEM((span, LANES), F32)
     four = pltpu.VMEM((4, span, LANES), F32)
     return pl.pallas_call(
-        functools.partial(terms_kernel, blocks),
+        functools.partial(viscous_terms, blocks),
         out_shape=(
             jax.ShapeDtypeStruct((3, span, LANES), F32),
             jax.ShapeDtypeStruct((2, span, LANES), F32),
@@ -241,41 +262,27 @@
         ),
         in_specs=in_vmem(2),
         out_specs=tuple(in_vmem(5)),
-        scratch_shapes=[square] * 5 + [four, four, pltpu.VMEM((4, LANES, LANES), F32)],
+        scratch_shapes=[square] * 5
+        + [four, four, pltpu.VMEM((4, LANES, LANES), F32)],
         compiler_params=vmem(8),
-        cost_estimate=work(4 * 1024 * 1024, 1024 * 1024),
-        name="viscous_terms",
+        cost_estimate=work(4 * MIB, MIB),
+        name="block_terms",
     )(lower, upper)
 
 
-def chunk_copy(source, target, sem, c):
-    rows = source.shape[0] // CHUNKS
-    where = pl.ds(c * rows, rows)
-    return pltpu.make_async_copy(source.at[where], target.at[where], sem.at[c])
-
-
-def start_all(source, target, sem):
-    for c in range(CHUNKS):
-        chunk_copy(source, target, sem, c).start()
-
-
-def streamed(shape, count):
-    return [pltpu.VMEM(shape, F32)] * count
-
-
-def rim_kernel(v_hbm, first_ref, last_ref, v_buf, sem):
-    span, planes, width = v_buf.shape
+def rim_kernel(v_hbm, v_ref, first_ref, last_ref, v_sem):
+    span, planes, width = v_ref.shape
     rows = span // CHUNKS
-    start_all(v_hbm, v_buf, sem)
+    start_all(v_hbm, v_ref, v_sem)
     lane = lane_of((planes, width))
     zero = jnp.zeros((planes, width), F32)
 
     def step(c, carry):
         first, last = carry
-        chunk_copy(v_hbm, v_buf, sem, c).wait()
+        chunk_copy(v_hbm, v_ref, v_sem, c).wait()
         for r in range(rows):
             i = c * rows + r
-            turned = pltpu.roll(v_buf[i], i, 1)
+            turned = pltpu.roll(v_ref[i], i, 1)
             first = jnp.where(lane == i, turned, first)
             last = jnp.where(lane == lax.rem(i + width - 1, width), turned, last)
         return (first, last)
@@ -290,27 +297,25 @@
     column = jax.ShapeDtypeStruct((planes, width), F32)
     return pl.pallas_call(
         rim_kernel,
-        out_shape=(column, column),
+        out_shape=(pltpu.VMEM(velocity.shape, F32), column, column),
         in_specs=in_hbm(1),
-        out_specs=tuple(in_vmem(2)),
-        scratch_shapes=streamed(velocity.shape, 1) + [pltpu.SemaphoreType.DMA((CHUNKS,))],
+        out_specs=tuple(in_vmem(3)),
+        scratch_shapes=[pltpu.SemaphoreType.DMA((CHUNKS,))],
         compiler_params=vmem(8),
         name="rim_columns",
     )(velocity)
 
 
-def sums_kernel(table, v_hbm, weight, vec_ref, v_buf, sem):
-    span, planes, width = v_buf.shape
+def sums_kernel(table, v_ref, weight, vec_ref):
+    span, planes, width = v_ref.shape
     rows = span // CHUNKS
-    start_all(v_hbm, v_buf, sem)
     zero = jnp.zeros((planes, width), F32)
 
     def step(c, carry):
         a, b, s, t = carry
-        chunk_copy(v_hbm, v_buf, sem, c).wait()
         for r in range(rows):
             i = c * rows + r
-            v = v_buf[i]
+            v = v_ref[i]
             a = a + weight[0, pl.ds(i, 1), :] * v
             b = b + weight[1, pl.ds(i, 1), :] * v
             s = s + table[4, i] * v
@@ -320,8 +325,8 @@
     sums = lax.fori_loop(0, CHUNKS, step, (zero, zero, zero, zero))
     for at in range(4):
         vec_ref[at] = sums[at]
-    vec_ref[4] = v_buf[0]
-    vec_ref[5] = v_buf[span - 1]
+    vec_ref[4] = v_ref[0]
+    vec_ref[5] = v_ref[span - 1]
 
 
 def local_sums(table, velocity, weight):
@@ -329,9 +334,8 @@
     return pl.pallas_call(
         sums_kernel,
         out_shape=jax.ShapeDtypeStruct((6, planes, width), F32),
-        in_specs=in_smem(1) + in_hbm(1) + in_vmem(1),
+        in_specs=in_smem(1) + in_vmem(2),
         out_specs=in_vmem(1)[0],
-        scratch_shapes=streamed(velocity.shape, 1) + [pltpu.SemaphoreType.DMA((CHUNKS,))],
         compiler_params=vmem(8),
         cost_estimate=work(8 * velocity.size, 4 * velocity.size),
         name="local_sums",
@@ -418,6 +422,7 @@
     cross_ref,
     order,
     out_hbm,
+    kept,
     v_ref,
     upd,
     even,
@@ -439,7 +444,9 @@
 
     def forward(i, r, vis):
         v = v_ref[i]
-        rim = pltpu.roll((odd if r % 2 else even)[...], lax.rem(width - i, width), 1)
+        rim = (odd if r % 2 else even)[...]
+        if r:
+            rim = pltpu.roll(rim, width - r, 1)
         low = jnp.where(lane == 0, rim, pltpu.roll(v, 1, 1))
         high = jnp.where(lane == width - 1, rim, pltpu.roll(v, width - 1, 1))
         rhs = keep * v + cross * (low + high)
@@ -451,39 +458,52 @@
         chunk_copy(v_hbm, v_ref, v_sem, c).wait()
         for r in range(rows):
             vis = forward(c * rows + r, r, vis)
+        even[...] = pltpu.roll(even[...], width - rows, 1)
+        odd[...] = pltpu.roll(odd[...], width - rows, 1)
         return vis
 
     lax.fori_loop(0, CHUNKS, down, zero)
 
+    base = (CHUNKS - KEPT) * rows
+
     def backward(i, vis):
-        vis = upd[i] + line[2, pl.ds(i, 1), :] * vis
-        upd[i] = vis
-        return vis
-
-    def up(step, vis):
-        c = CHUNKS - 1 - step
-        for r in range(rows - 1, -1, -1):
-            vis = backward(c * rows + r, vis)
-        chunk_copy(upd, out_hbm, out_sem, c).start()
-        return vis
-
-    upd[inner] = zero
+        return upd[i] + line[2, pl.ds(i, 1), :] * vis
+
+    kept[inner - base] = zero
     vis = zero
     for i in range(inner - 1, span - 1 - rows, -1):
         vis = backward(i, vis)
-    chunk_copy(upd, out_hbm, out_sem, CHUNKS - 1).start()
-    lax.fori_loop(1, CHUNKS, up, vis)
-    for c in range(CHUNKS):
-        chunk_copy(upd, out_hbm, out_sem, c).wait()
+        kept[i - base] = vis
+
+    def keep_chunk(step, vis):
+        for r in range(rows - 1, -1, -1):
+            i = (CHUNKS - 1 - step) * rows + r
+            vis = backward(i, vis)
+            kept[i - base] = vis
+        return vis
+
+    vis = lax.fori_loop(1, KEPT, keep_chunk, vis)
+    for c in range(CHUNKS - KEPT - 1, -1, -1):
+        for r in range(rows - 1, -1, -1):
+            i = c * rows + r
+            vis = backward(i, vis)
+            upd[i] = vis
+        row_copy(upd, out_hbm, out_sem, c, rows).start()
+    for c in range(CHUNKS - KEPT):
+        row_copy(upd, out_hbm, out_sem, c, rows).wait()
 
 
 def viscous_solve(velocity, line, before, after, cross, order):
     span, planes, width = velocity.shape
+    kept = KEPT * (span // CHUNKS)
     return pl.pallas_call(
         viscous_kernel,
-        out_shape=pltpu.HBM(velocity.shape, F32),
+        out_shape=(
+            pltpu.HBM((span - kept, planes, width), F32),
+            pltpu.VMEM((kept, planes, width), F32),
+        ),
         in_specs=in_hbm(1) + in_vmem(4) + [pl.BlockSpec(memory_space=pl.ANY)],
-        out_specs=in_hbm(1)[0],
+        out_specs=tuple(in_hbm(1) + in_vmem(1)),
         scratch_shapes=streamed(velocity.shape, 2)
         + [pltpu.VMEM((planes, width), F32)] * 2
         + [pltpu.SemaphoreType.DMA((CHUNKS,))] * 2,
@@ -514,15 +534,8 @@
     vectors += [vec_ref[at] for at in range(2, 6)]
     for at, value in enumerate(vectors):
         for m in range(blocks):
-            out_ref[m, part * at : part * (at + 1), :] = value[part * m : part * (m + 1), :]
-    rest = out_ref.shape[1] - 6 * part
-    if rest:
-        out_ref[:, 6 * part :, :] = jnp.zeros((blocks, rest, out_ref.shape[2]), F32)
+            out_ref[m, at] = value[part * m : part * (m + 1), :]
     token[...] = jnp.zeros(token.shape, F32)
-
-
-def rows_sent(part):
-    return -(-6 * part // 8) * 8
 
 
 def pack(vec, row, before, after, cross, blocks):
@@ -530,18 +543,18 @@
     part = planes // blocks
     return pl.pallas_call(
         pack_kernel,
-        out_shape=(jax.ShapeDtypeStruct((blocks, rows_sent(part), width), F32), TOKEN),
+        out_shape=(jax.ShapeDtypeStruct((blocks, 6, part, width), F32), TOKEN),
         compiler_params=vmem(8),
         name="pack_sums",
     )(vec, row, before, after, cross)
 
 
-def reduced_kernel(part, red, weights, coef_ref, in_ref, order, out_ref, token):
-    blocks, rows, width = in_ref.shape
+def reduced_kernel(red, weights, coef_ref, in_ref, order, out_ref, token):
+    blocks, _, part, width = in_ref.shape
     slope_after, slope_before = (weights["after"], weights["before"])
 
     def piece(k, at):
-        return in_ref[k, part * at : part * (at + 1), :]
+        return in_ref[k, at]
 
     zero = jnp.zeros((part, width), F32)
     vis, slo = (zero, zero)
@@ -563,28 +576,25 @@
         vis_all.append(vis)
         slo_all.append(slo)
     vis, slo = (zero, zero)
-    rest = rows - 6 * part
     for k in range(blocks - 1, -1, -1):
         vis = vis_all[k] + coef_ref[2, k : k + 1, :] * vis
         slo = slo_all[k] + red[k][2] * slo
-        out_ref[k, part : 2 * part, :] = vis
-        out_ref[k, 3 * part : 4 * part, :] = slo
+        out_ref[k, 1] = vis
+        out_ref[k, 3] = slo
         if k < blocks - 1:
-            out_ref[k + 1, 0:part, :] = vis
-            out_ref[k + 1, 2 * part : 3 * part, :] = slo + (BODY / ALPHA) * piece(k, 5)
+            out_ref[k + 1, 0] = vis
+            out_ref[k + 1, 2] = slo + (BODY / ALPHA) * piece(k, 5)
         else:
-            out_ref[0, 0:part, :] = zero
-            out_ref[0, 2 * part : 3 * part, :] = zero
-        out_ref[k, 4 * part : 5 * part, :] = piece(k - 1, 5) if k > 0 else zero
-        out_ref[k, 5 * part : 6 * part, :] = piece(k + 1, 4) if k < blocks - 1 else zero
-    if rest:
-        out_ref[:, 6 * part :, :] = jnp.zeros((blocks, rest, width), F32)
+            out_ref[0, 0] = zero
+            out_ref[0, 2] = zero
+        out_ref[k, 4] = piece(k - 1, 5) if k > 0 else zero
+        out_ref[k, 5] = piece(k + 1, 4) if k < blocks - 1 else zero
     token[...] = jnp.zeros(token.shape, F32)
 
 
-def reduced_solve(coef, arrived, order, red, weights, part):
+def reduced_solve(coef, arrived, order, red, weights):
     return pl.pallas_call(
-        functools.partial(reduced_kernel, part, red, weights),
+        functools.partial(reduced_kernel, red, weights),
         out_shape=(jax.ShapeDtypeStruct(arrived.shape, F32), TOKEN),
         in_specs=in_vmem(2) + in_hbm(1),
         out_specs=tuple(in_vmem(2)),
@@ -598,6 +608,7 @@
     metric,
     der_in,
     upd_in,
+    kept,
     edge_ref,
     spike,
     der_hbm,
@@ -614,83 +625,95 @@
     blocks = edge_ref.shape[0]
     part = planes // blocks
     rows = span // CHUNKS
-    for c in range(CHUNKS):
-        chunk_copy(der_in, der, der_from, c).start()
-        chunk_copy(upd_in, upd, upd_from, c).start()
+    far = CHUNKS - KEPT
+    for c in range(CHUNKS - 1, -1, -1):
+        row_copy(der_in, der, der_from, c, rows).start()
+    for c in range(far - 1, -1, -1):
+        row_copy(upd_in, upd, upd_from, c, rows).start()
     for at in range(6):
         for m in range(blocks):
-            edges[at, part * m : part * (m + 1), :] = edge_ref[m, part * at : part * (at + 1), :]
+            edges[at, part * m : part * (m + 1), :] = edge_ref[m, at]
     vis_low, vis_high, slo_low, slo_high = (edges[at] for at in range(4))
 
-    def step(c, carry):
-        chunk_copy(der_in, der, der_from, c).wait()
-        chunk_copy(upd_in, upd, upd_from, c).wait()
+    def viscous_rows(c, source, base):
+        for r in range(rows):
+            i = c * rows + r
+            low = spike[0, pl.ds(i, 1), :] * vis_low
+            high = spike[1, pl.ds(i, 1), :] * vis_high
+            upd[i] = source[i - base] + low + high
+        row_copy(upd, upd_hbm, upd_to, c, rows).start()
+
+    def slope_rows(c):
+        row_copy(der_in, der, der_from, c, rows).wait()
         for r in range(rows):
             i = c * rows + r
             scale = metric[i]
             der[i] = der[i] + (scale * table[6, i]) * slo_low + (scale * table[7, i]) * slo_high
-            upd[i] = (
-                upd[i] + spike[0, pl.ds(i, 1), :] * vis_low + spike[1, pl.ds(i, 1), :] * vis_high
-            )
         if isinstance(c, int) and c == 0:
             der[0] = der[0] - (metric[0] * DIRECT) * edges[4]
         if isinstance(c, int) and c == CHUNKS - 1:
             der[span - 1] = der[span - 1] + (metric[span - 1] * DIRECT) * edges[5]
-        chunk_copy(der, der_hbm, der_to, c).start(priority=1)
-        chunk_copy(upd, upd_hbm, upd_to, c).start(priority=1)
+        row_copy(der, der_hbm, der_to, c, rows).start()
+
+    def near(step, carry):
+        viscous_rows(CHUNKS - 1 - step, kept, far * rows)
+        slope_rows(CHUNKS - 1 - step)
         return carry
 
-    step(0, 0)
-    lax.fori_loop(1, CHUNKS - 1, step, 0)
-    step(CHUNKS - 1, 0)
+    viscous_rows(CHUNKS - 1, kept, far * rows)
+    slope_rows(CHUNKS - 1)
+    lax.fori_loop(1, KEPT, near, 0)
+    for c in range(far - 1, -1, -1):
+        row_copy(upd_in, upd, upd_from, c, rows).wait()
+        viscous_rows(c, upd, 0)
+        slope_rows(c)
     for c in range(CHUNKS):
-        chunk_copy(der, der_hbm, der_to, c).wait()
-        chunk_copy(upd, upd_hbm, upd_to, c).wait()
-
-
-def final_solve(table, metric, der, upd, edge, spike):
+        row_copy(der, der_hbm, der_to, c, rows).wait()
+        row_copy(upd, upd_hbm, upd_to, c, rows).wait()
+
+
+def final_solve(table, metric, der, upd, kept, edge, spike):
     span, planes, width = der.shape
     result = jax.ShapeDtypeStruct(der.shape, F32)
     return pl.pallas_call(
         final_kernel,
         out_shape=(result, result),
-        in_specs=in_smem(2) + in_hbm(2) + in_vmem(2),
+        in_specs=in_smem(2) + in_hbm(2) + in_vmem(3),
         out_specs=tuple(in_hbm(2)),
         scratch_shapes=streamed(der.shape, 2)
         + [pltpu.VMEM((6, planes, width), F32)]
         + [pltpu.SemaphoreType.DMA((CHUNKS,))] * 4,
-        compiler_params=vmem(16),
+        compiler_params=vmem(12),
         name="final_solve",
-    )(table, metric, der, upd, edge, spike)
+    )(table, metric, der, upd, kept, edge, spike)
 
 
 def body(velocity, metric, lower_coupling, upper_coupling, cross_diffusion):
     span, planes, width = velocity.shape
     blocks = lax.axis_size("gx")
     walls = lax.axis_size("gy")
-    part = planes // blocks
     rows, red, weights = slope_constants(blocks, span)
     table = jnp.asarray(rows)
     cross = cross_diffusion.reshape(1, width)
-    line, weight, spike, row, coef = viscous_terms(
-        lower_coupling.reshape(blocks, span), upper_coupling.reshape(blocks, span)
-    )
     field = pltpu.with_memory_space_constraint(velocity, pltpu.HBM)
-    first, last = rim_columns(field)
+    lower = lower_coupling.reshape(blocks, span)
+    upper = upper_coupling.reshape(blocks, span)
+    near, first, last = rim_columns(field)
     up = [(j, j + 1) for j in range(walls - 1)]
     down = [(j + 1, j) for j in range(walls - 1)]
     before = lax.ppermute(last, "gy", up)
     after = lax.ppermute(first, "gy", down)
-    vec = local_sums(table, field, weight)
+    line, weight, spike, row, coef = block_terms(lower, upper)
+    vec = local_sums(table, near, weight)
     packed, token = pack(vec, row, before, after, cross, blocks)
     arrived = lax.all_to_all(packed, "gx", 0, 0, tiled=True)
     der = slope_solve(table, metric, field, token)
     der = pltpu.with_memory_space_constraint(der, pltpu.HBM)
-    solved, token = reduced_solve(coef, arrived, der, red, weights, part)
+    solved, token = reduced_solve(coef, arrived, der, red, weights)
     edge = lax.all_to_all(solved, "gx", 0, 0, tiled=True)
-    upd = viscous_solve(field, line, before, after, cross, token)
+    upd, kept = viscous_solve(field, line, before, after, cross, token)
     upd = pltpu.with_memory_space_constraint(upd, pltpu.HBM)
-    return final_solve(table, metric, der, upd, edge, spike)
+    return final_solve(table, metric, der, upd, kept, edge, spike)
 
 
 def solution(mesh):

time: 54.9 us -> 52.8 us (0.962)
  Pallas kernels: 28.3 us -> 25.4 us
    ppermute x1, waiting for transfers between devices: 0.01 us -> 1.18 us  [body(): after = lax.ppermute(first, 'gy', down)]
    pallas_call x1, Pallas kernels: 2.97 us -> 1.81 us  [local_sums(): pl.pallas_call(sums_kernel, out_shape=jax.ShapeDtypeStruct((6, planes, wi...]
    pallas_call x1, Pallas kernels: 7.6 us -> 6.51 us  [final_solve(): pl.pallas_call(final_kernel, out_shape=(result, result), in_specs=in_smem...]
    all_to_all x1, waiting for transfers between devices: 3.84 us -> 3.17 us  [body(): arrived = lax.all_to_all(packed, 'gx', 0, 0, tiled=True)]
    pallas_call x5, Pallas kernels: 12.6 us -> 11.9 us  [the longest x1 6.47 us: viscous_solve(): pl.pallas_call(viscous_kernel, out_shape=(pltpu.HBM((span - kept, planes,...]
  transfers between devices with their start and end apart: 4 -> 4, of which waited for: 2 -> 3; matrix products, arithmetic and copies ran while one was open for 0% -> 0% of each run, Pallas kernels for 29% -> 27%
where the time goes in v1:
time: 52.8 us; the launch traced here: 52.5 us
  Pallas kernels  25.4 us (48%)
  starting transfers between devices  20.1 us (38%)
  waiting for transfers between devices  6.21 us (12%)
  between operations  0.76 us (1%)
    all_to_all x1, starting transfers between devices, body(): arrived = lax.all_to_all(packed, 'gx', 0, 0, tiled=True)  9.19 us
    pallas_call x1, Pallas kernels, final_solve(): pl.pallas_call(final_kernel, out_shape=(result, result), in_specs=in_smem...  6.51 us
    pallas_call x1, Pallas kernels, viscous_solve(): pl.pallas_call(viscous_kernel, out_shape=(pltpu.HBM((span - kept, planes,...  6.47 us
    pallas_call x1, Pallas kernels, slope_solve(): pl.pallas_call(slope_kernel, out_shape=pltpu.HBM(velocity.shape, F32), in...  5.14 us
    ppermute x1, starting transfers between devices, body(): before = lax.ppermute(last, 'gy', up)  4.76 us
    all_to_all x1, starting transfers between devices, body(): edge = lax.all_to_all(solved, 'gx', 0, 0, tiled=True)  4.22 us
    all_to_all x1, waiting for transfers between devices, body(): arrived = lax.all_to_all(packed, 'gx', 0, 0, tiled=True)  3.17 us
    pallas_call x1, Pallas kernels, rim_columns(): pl.pallas_call(rim_kernel, out_shape=(pltpu.VMEM(velocity.shape, F32), co...  2.85 us
  transfers between devices with their start and end apart: 4, of which 3 were waited for; matrix products, arithmetic and copies ran while one was open for 0% of the time, Pallas kernels for 27%

profile of v1, /device:TPU:97, one launch (start us, length us, event | category | flops | bytes accessed | tf_op | source)
XLA Modules:
  0.0 52.5 jit_solution(13627856937503704535)
XLA Ops:
  0.6 0.0 copy-start
  0.6 0.0 copy-start.2
  0.7 0.0 copy-start.1
  0.7 0.0 copy-start.4
  0.7 0.0 copy-start.3
  0.7 2.8 %rim_columns.1 = (f32[128,64,128]{2,1,0:T(8,128)S(1)}, f32[64,128]{1,0:T(8,128)S(1)}, f32[64,128]{1,0:T(8,128)S(1)}) custom-call(f32[128,64,128]{2,1,0:T(8,128)} %v_hbm.5), custom_call_target="tpu_custom_call" | custom-call | tf_op jit(solution)/shard_map/rim_columns/pallas_call | solution.py:298
  3.5 4.8 %collective-permute-start = (f32[64,128]{1,0:T(8,128)S(1)}, f32[64,128]{1,0:T(8,128)S(1)}, u32[]{:S(2)}, u32[]{:S(2)}) collective-permute-start(f32[64,128]{1,0:T(8,128)S(1)} %get-tuple-element.19), channel_id=1, source_target_pairs={{0,1},{1,2},{2,3},{3,4},{4,5},{5,6},{6,7},{8,9},{9,10},{10,11},{11... | collective-permute-start | bytes 98312 | tf_op jit(solution)/shard_map/ppermute | solution.py:704
  8.3 1.9 %collective-permute-start.1 = (f32[64,128]{1,0:T(8,128)S(1)}, f32[64,128]{1,0:T(8,128)S(1)}, u32[]{:S(2)}, u32[]{:S(2)}) collective-permute-start(f32[64,128]{1,0:T(8,128)S(1)} %get-tuple-element.20), channel_id=1, source_target_pairs={{1,0},{2,1},{3,2},{4,3},{5,4},{6,5},{7,6},{9,8},{10,9},{11,10},{12... | collective-permute-start | bytes 98312 | tf_op jit(solution)/shard_map/ppermute | solution.py:705
  10.2 0.0 copy-done.2
  10.2 0.0 copy-done.1
  10.2 0.9 %block_terms.1 = (f32[3,128,128]{2,1,0:T(8,128)S(1)}, f32[2,128,128]{2,1,0:T(8,128)S(1)}, f32[2,128,128]{2,1,0:T(8,128)S(1)}, f32[2,8,128]{2,1,0:T(8,128)S(1)}, f32[3,32,128]{2,1,0:T(8,128)S(1)}) custom-call(f32[32,128]{1,0:T(8,128)S(1)} %bitcast.3, f32[32,128]{1,0:T(8,128)S(1)} %bitcast.4), custom_call_target="tpu_custom_call" | custom-call | flops 4194304 | bytes 1048576 | tf_op jit(solution)/shard_map/block_terms/pallas_call | solution.py:254
  11.2 0.0 copy-done
  11.2 1.8 %local_sums.1.vec_ref = f32[6,64,128]{2,1,0:T(8,128)S(1)} custom-call(f32[8,128]{1,0:T(8,128)S(1)} %copy-done, f32[128,64,128]{2,1,0:T(8,128)S(1)} %get-tuple-element.16.v_ref, f32[2,128,128]{2,1,0:T(8,128)S(1)} %get-tuple-element.17.weight), custom_call_target="tpu_custom_call" | custom-call | flops 8388608 | bytes 4194304 | tf_op jit(solution)/shard_map/local_sums/pallas_call | solution.py:334
  13.0 0.0 collective-permute-done.before_ref
  13.0 1.2 %collective-permute-done.1.after_ref = f32[64,128]{1,0:T(8,128)S(1)} collective-permute-done((f32[64,128]{1,0:T(8,128)S(1)}, f32[64,128]{1,0:T(8,128)S(1)}, u32[]{:S(2)}, u32[]{:S(2)}) %collective-permute-start.1) | collective-permute-done | bytes 32800 | tf_op jit(solution)/shard_map/ppermute | solution.py:705
  14.2 0.8 %pack_sums.1 = (f32[32,6,2,128]{3,2,1,0:T(2,128)}, f32[8,128]{1,0:T(8,128)S(1)}) custom-call(f32[6,64,128]{2,1,0:T(8,128)S(1)} %local_sums.1.vec_ref, f32[2,8,128]{2,1,0:T(8,128)S(1)} %get-tuple-element.18.row_ref, f32[64,128]{1,0:T(8,128)S(1)} %collective-permute-done.before_ref, f32[64,128]{1,0:T(8,128)S(1)} %collective-permute-done.1.after_ref, ...), custom_call_target="tpu_custom_call" | custom-call | tf_op jit(solution)/shard_map/pack_sums/pallas_call | solution.py:544
  15.0 9.2 %all-to-all-start = ((f32[32,6,2,128]{3,2,1,0:T(2,128)}), f32[32,6,2,128]{3,2,1,0:T(2,128)S(1)}, u32[]{:S(2)}, u32[]{:S(2)}) async-start(f32[32,6,2,128]{3,2,1,0:T(2,128)} %get-tuple-element.24), calls=%async_computation | async-start | bytes 393216 | tf_op jit(solution)/shard_map/all_to_all | solution.py:709
  24.2 5.1 %slope_solve.1.order.der_in = f32[128,64,128]{2,1,0:T(8,128)} custom-call(f32[8,128]{1,0:T(8,128)S(1)} %copy-done, f32[128]{0:T(128)S(1)} %copy-done.3, f32[128,64,128]{2,1,0:T(8,128)} %v_hbm.5, f32[8,128]{1,0:T(8,128)S(1)} %get-tuple-element.21.order), custom_call_target="tpu_custom_call" | custom-call | flops 12582912 | bytes 12582912 | tf_op jit(solution)/shard_map/slope_solve/pallas_call | solution.py:405
  29.4 3.2 %all-to-all-done.in_ref = f32[32,6,2,128]{3,2,1,0:T(2,128)S(1)} async-done(((f32[32,6,2,128]{3,2,1,0:T(2,128)}), f32[32,6,2,128]{3,2,1,0:T(2,128)S(1)}, u32[]{:S(2)}, u32[]{:S(2)}) %all-to-all-start) | async-done | bytes 196640 | tf_op jit(solution)/shard_map/all_to_all | solution.py:709
  32.5 0.9 %reduced_solve.1 = (f32[32,6,2,128]{3,2,1,0:T(2,128)}, f32[8,128]{1,0:T(8,128)S(1)}) custom-call(f32[3,32,128]{2,1,0:T(8,128)S(1)} %get-tuple-element.23.coef_ref, f32[32,6,2,128]{3,2,1,0:T(2,128)S(1)} %all-to-all-done.in_ref, f32[128,64,128]{2,1,0:T(8,128)} %slope_solve.1.order.der_in), custom_call_target="tpu_custom_call" | custom-call | tf_op jit(solution)/shard_map/reduced_solve/pallas_call | solution.py:596
  33.4 4.2 %all-to-all-start.1 = ((f32[32,6,2,128]{3,2,1,0:T(2,128)}), f32[32,6,2,128]{3,2,1,0:T(2,128)S(1)}, u32[]{:S(2)}, u32[]{:S(2)}) async-start(f32[32,6,2,128]{3,2,1,0:T(2,128)} %get-tuple-element.28), calls=%async_computation.1 | async-start | bytes 393216 | tf_op jit(solution)/shard_map/all_to_all | solution.py:713
  37.6 6.5 %viscous_solve.1 = (f32[48,64,128]{2,1,0:T(8,128)}, f32[80,64,128]{2,1,0:T(8,128)S(1)}) custom-call(f32[128,64,128]{2,1,0:T(8,128)} %v_hbm.5, f32[3,128,128]{2,1,0:T(8,128)S(1)} %get-tuple-element.22.line, f32[64,128]{1,0:T(8,128)S(1)} %collective-permute-done.before_ref, f32[64,128]{1,0:T(8,128)S(1)} %collective-permute-done.1.after_ref, ...), custom_call_target="tpu_custom_call" | custom-call | flops 12582912 | bytes 12582912 | tf_op jit(solution)/shard_map/viscous_solve/pallas_call | solution.py:499
  44.1 1.9 %all-to-all-done.1.edge_ref = f32[32,6,2,128]{3,2,1,0:T(2,128)S(1)} async-done(((f32[32,6,2,128]{3,2,1,0:T(2,128)}), f32[32,6,2,128]{3,2,1,0:T(2,128)S(1)}, u32[]{:S(2)}, u32[]{:S(2)}) %all-to-all-start.1) | async-done | bytes 196640 | tf_op jit(solution)/shard_map/all_to_all | solution.py:713
  46.0 6.5 %final_solve.1 = (f32[128,64,128]{2,1,0:T(8,128)}, f32[128,64,128]{2,1,0:T(8,128)}) custom-call(f32[8,128]{1,0:T(8,128)S(1)} %copy-done, f32[128]{0:T(128)S(1)} %copy-done.3, f32[128,64,128]{2,1,0:T(8,128)} %slope_solve.1.order.der_in, f32[48,64,128]{2,1,0:T(8,128)} %get-tuple-element.26.upd_in, f32[80,64,128]{2,1,0:T(8,128)S(1)} %get-tuple-element.27.kept, ...), custom_call_target="tpu_custom_call" | custom-call | tf_op jit(solution)/shard_map/final_solve/pallas_call | solution.py:678
  (2 shorter events, 0.0 us)
Async XLA Ops:
  0.6 10.5 %copy-start = (f32[8,128]{1,0:T(8,128)S(1)}, f32[8,128]{1,0:T(8,128)}, u32[]{:S(2)}) copy-start(f32[8,128]{1,0:T(8,128)} %constant.2.clone.table) | copy-start | bytes 12292
  0.6 9.6 %copy-start.2 = (f32[4096]{0:T(1024)S(1)}, f32[4096]{0:T(1024)}, u32[]{:S(2)}) copy-start(f32[4096]{0:T(1024)} %param.9) | copy-start | bytes 49156
  0.7 9.6 %copy-start.1 = (f32[4096]{0:T(1024)S(1)}, f32[4096]{0:T(1024)}, u32[]{:S(2)}) copy-start(f32[4096]{0:T(1024)} %param.8) | copy-start | bytes 49156
  0.7 13.5 %copy-start.4 = (f32[128]{0:T(128)S(1)}, f32[128]{0:T(128)}, u32[]{:S(2)}) copy-start(f32[128]{0:T(128)} %param.10) | copy-start | bytes 1540
  0.7 23.5 %copy-start.3 = (f32[128]{0:T(128)S(1)}, f32[128]{0:T(128)}, u32[]{:S(2)}) copy-start(f32[128]{0:T(128)} %metric.3) | copy-start | bytes 1540
  3.5 9.4 %collective-permute-start = (f32[64,128]{1,0:T(8,128)S(1)}, f32[64,128]{1,0:T(8,128)S(1)}, u32[]{:S(2)}, u32[]{:S(2)}) collective-permute-start(f32[64,128]{1,0:T(8,128)S(1)} %get-tuple-element.19), channel_id=1, source_target_pairs={{0,1},{1,2},{2,3},{3,4},{4,5},{5,6},{6,7},{8,9},{9,10},{10,11},{11... | collective-permute-start | bytes 98312 | tf_op jit(solution)/shard_map/ppermute | solution.py:704
  8.3 5.9 %collective-permute-start.1 = (f32[64,128]{1,0:T(8,128)S(1)}, f32[64,128]{1,0:T(8,128)S(1)}, u32[]{:S(2)}, u32[]{:S(2)}) collective-permute-start(f32[64,128]{1,0:T(8,128)S(1)} %get-tuple-element.20), channel_id=1, source_target_pairs={{1,0},{2,1},{3,2},{4,3},{5,4},{6,5},{7,6},{9,8},{10,9},{11,10},{12... | collective-permute-start | bytes 98312 | tf_op jit(solution)/shard_map/ppermute | solution.py:705
  15.0 17.5 %all-to-all-start = ((f32[32,6,2,128]{3,2,1,0:T(2,128)}), f32[32,6,2,128]{3,2,1,0:T(2,128)S(1)}, u32[]{:S(2)}, u32[]{:S(2)}) async-start(f32[32,6,2,128]{3,2,1,0:T(2,128)} %get-tuple-element.24), calls=%async_computation | async-start | bytes 393216 | tf_op jit(solution)/shard_map/all_to_all | solution.py:709
  33.4 12.6 %all-to-all-start.1 = ((f32[32,6,2,128]{3,2,1,0:T(2,128)}), f32[32,6,2,128]{3,2,1,0:T(2,128)S(1)}, u32[]{:S(2)}, u32[]{:S(2)}) async-start(f32[32,6,2,128]{3,2,1,0:T(2,128)} %get-tuple-element.28), calls=%async_computation.1 | async-start | bytes 393216 | tf_op jit(solution)/shard_map/all_to_all | solution.py:713

commit v2 on v1

--- a/solution.py
+++ b/solution.py
@@ -15,7 +15,7 @@
 END = 1.0 / 36.0
 LANES = 128
 CHUNKS = 8
-KEPT = 5
+KEPT = 6
 MIB = 1024 * 1024
 F32 = jnp.float32
 TOKEN = jax.ShapeDtypeStruct((8, LANES), F32)
@@ -216,11 +216,12 @@
         column = jnp.sum(jnp.where(lane == index, value, 0.0), axis=1, keepdims=True)
         return jnp.broadcast_to(column, (span, LANES))
 
-    line_ref[0] = mine(rho)
-    line_ref[1] = mine(mu)
-    line_ref[2] = mine(nu)
-    spike_ref[0] = mine(chain[2])
-    spike_ref[1] = mine(chain[3])
+    for at, value in enumerate((rho, mu, nu)):
+        turn[at] = jnp.transpose(value)
+        line_ref[at : at + 1, :] = turn[at, pl.ds(index, 1), :]
+    for at in range(2):
+        turn[at] = jnp.transpose(chain[2 + at])
+        spike_ref[at : at + 1, :] = turn[at, pl.ds(index, 1), :]
     for at, value in enumerate((own, first)):
         here = mine(value)
         weight_ref[at] = here
@@ -254,9 +255,9 @@
     return pl.pallas_call(
         functools.partial(viscous_terms, blocks),
         out_shape=(
-            jax.ShapeDtypeStruct((3, span, LANES), F32),
+            jax.ShapeDtypeStruct((3, span), F32),
             jax.ShapeDtypeStruct((2, span, LANES), F32),
-            jax.ShapeDtypeStruct((2, span, LANES), F32),
+            jax.ShapeDtypeStruct((2, span), F32),
             jax.ShapeDtypeStruct((2, 8, span), F32),
             jax.ShapeDtypeStruct((3, blocks, LANES), F32),
         ),
@@ -450,7 +451,7 @@
         low = jnp.where(lane == 0, rim, pltpu.roll(v, 1, 1))
         high = jnp.where(lane == width - 1, rim, pltpu.roll(v, width - 1, 1))
         rhs = keep * v + cross * (low + high)
-        vis = line[0, pl.ds(i, 1), :] * rhs + line[1, pl.ds(i, 1), :] * vis
+        vis = line[0, i] * rhs + line[1, i] * vis
         upd[i] = vis
         return vis
 
@@ -467,7 +468,7 @@
     base = (CHUNKS - KEPT) * rows
 
     def backward(i, vis):
-        return upd[i] + line[2, pl.ds(i, 1), :] * vis
+        return upd[i] + line[2, i] * vis
 
     kept[inner - base] = zero
     vis = zero
@@ -502,7 +503,7 @@
             pltpu.HBM((span - kept, planes, width), F32),
             pltpu.VMEM((kept, planes, width), F32),
         ),
-        in_specs=in_hbm(1) + in_vmem(4) + [pl.BlockSpec(memory_space=pl.ANY)],
+        in_specs=in_hbm(1) + in_smem(1) + in_vmem(3) + [pl.BlockSpec(memory_space=pl.ANY)],
         out_specs=tuple(in_hbm(1) + in_vmem(1)),
         scratch_shapes=streamed(velocity.shape, 2)
         + [pltpu.VMEM((planes, width), F32)] * 2
@@ -638,8 +639,8 @@
     def viscous_rows(c, source, base):
         for r in range(rows):
             i = c * rows + r
-            low = spike[0, pl.ds(i, 1), :] * vis_low
-            high = spike[1, pl.ds(i, 1), :] * vis_high
+            low = spike[0, i] * vis_low
+            high = spike[1, i] * vis_high
             upd[i] = source[i - base] + low + high
         row_copy(upd, upd_hbm, upd_to, c, rows).start()
 
@@ -678,7 +679,7 @@
     return pl.pallas_call(
         final_kernel,
         out_shape=(result, result),
-        in_specs=in_smem(2) + in_hbm(2) + in_vmem(3),
+        in_specs=in_smem(2) + in_hbm(2) + in_vmem(2) + in_smem(1),
         out_specs=tuple(in_hbm(2)),
         scratch_shapes=streamed(der.shape, 2)
         + [pltpu.VMEM((6, planes, width), F32)]

time: 52.8 us -> 52.3 us (level)
  transfers between devices with their start and end apart: 4 -> 4, of which waited for: 3 -> 3; matrix products, arithmetic and copies ran while one was open for 0% -> 0% of each run, Pallas kernels for 27% -> 28%
where the time goes in v2:
time: 52.3 us; the launch traced here: 52 us
  Pallas kernels  25.3 us (48%)
  starting transfers between devices  20.1 us (38%)
  waiting for transfers between devices  5.81 us (11%)
  between operations  0.78 us (1%)
    all_to_all x1, starting transfers between devices, body(): arrived = lax.all_to_all(packed, 'gx', 0, 0, tiled=True)  9.19 us
    pallas_call x1, Pallas kernels, viscous_solve(): pl.pallas_call(viscous_kernel, out_shape=(pltpu.HBM((span - kept, planes,...  6.91 us
    pallas_call x1, Pallas kernels, final_solve(): pl.pallas_call(final_kernel, out_shape=(result, result), in_specs=in_smem...  5.99 us
    pallas_call x1, Pallas kernels, slope_solve(): pl.pallas_call(slope_kernel, out_shape=pltpu.HBM(velocity.shape, F32), in...  5.14 us
    ppermute x1, starting transfers between devices, body(): before = lax.ppermute(last, 'gy', up)  4.76 us
    all_to_all x1, starting transfers between devices, body(): edge = lax.all_to_all(solved, 'gx', 0, 0, tiled=True)  4.22 us
    all_to_all x1, waiting for transfers between devices, body(): arrived = lax.all_to_all(packed, 'gx', 0, 0, tiled=True)  3.17 us
    pallas_call x1, Pallas kernels, rim_columns(): pl.pallas_call(rim_kernel, out_shape=(pltpu.VMEM(velocity.shape, F32), co...  2.85 us
  transfers between devices with their start and end apart: 4, of which 3 were waited for; matrix products, arithmetic and copies ran while one was open for 0% of the time, Pallas kernels for 28%

profile of v2, /device:TPU:97, one launch (start us, length us, event | category | flops | bytes accessed | tf_op | source)
XLA Modules:
  0.0 52.0 jit_solution(12374543620893160869)
XLA Ops:
  0.6 0.0 copy-start
  0.6 0.0 copy-start.2
  0.7 0.0 copy-start.1
  0.7 0.0 copy-start.3
  0.7 0.0 copy-start.4
  0.7 2.8 %rim_columns.1 = (f32[128,64,128]{2,1,0:T(8,128)S(1)}, f32[64,128]{1,0:T(8,128)S(1)}, f32[64,128]{1,0:T(8,128)S(1)}) custom-call(f32[128,64,128]{2,1,0:T(8,128)} %v_hbm.5), custom_call_target="tpu_custom_call" | custom-call | tf_op jit(solution)/shard_map/rim_columns/pallas_call | solution.py:299
  3.5 4.8 %collective-permute-start = (f32[64,128]{1,0:T(8,128)S(1)}, f32[64,128]{1,0:T(8,128)S(1)}, u32[]{:S(2)}, u32[]{:S(2)}) collective-permute-start(f32[64,128]{1,0:T(8,128)S(1)} %get-tuple-element.19), channel_id=1, source_target_pairs={{0,1},{1,2},{2,3},{3,4},{4,5},{5,6},{6,7},{8,9},{9,10},{10,11},{11... | collective-permute-start | bytes 98312 | tf_op jit(solution)/shard_map/ppermute | solution.py:705
  8.3 1.9 %collective-permute-start.1 = (f32[64,128]{1,0:T(8,128)S(1)}, f32[64,128]{1,0:T(8,128)S(1)}, u32[]{:S(2)}, u32[]{:S(2)}) collective-permute-start(f32[64,128]{1,0:T(8,128)S(1)} %get-tuple-element.20), channel_id=1, source_target_pairs={{1,0},{2,1},{3,2},{4,3},{5,4},{6,5},{7,6},{9,8},{10,9},{11,10},{12... | collective-permute-start | bytes 98312 | tf_op jit(solution)/shard_map/ppermute | solution.py:706
  10.2 0.0 copy-done.2
  10.2 0.0 copy-done.1
  10.2 0.9 %block_terms.1 = (f32[3,128]{1,0:T(4,128)S(1)}, f32[2,128,128]{2,1,0:T(8,128)S(1)}, f32[2,128]{1,0:T(2,128)S(1)}, f32[2,8,128]{2,1,0:T(8,128)S(1)}, f32[3,32,128]{2,1,0:T(8,128)S(1)}) custom-call(f32[32,128]{1,0:T(8,128)S(1)} %bitcast.3, f32[32,128]{1,0:T(8,128)S(1)} %bitcast.4), custom_call_target="tpu_custom_call" | custom-call | flops 4194304 | bytes 1048576 | tf_op jit(solution)/shard_map/block_terms/pallas_call | solution.py:255
  11.1 0.0 copy-done
  11.1 1.8 %local_sums.1.vec_ref = f32[6,64,128]{2,1,0:T(8,128)S(1)} custom-call(f32[8,128]{1,0:T(8,128)S(1)} %copy-done, f32[128,64,128]{2,1,0:T(8,128)S(1)} %get-tuple-element.16.v_ref, f32[2,128,128]{2,1,0:T(8,128)S(1)} %get-tuple-element.17.weight), custom_call_target="tpu_custom_call" | custom-call | flops 8388608 | bytes 4194304 | tf_op jit(solution)/shard_map/local_sums/pallas_call | solution.py:335
  12.9 0.0 collective-permute-done.before_ref
  12.9 1.2 %collective-permute-done.1.after_ref = f32[64,128]{1,0:T(8,128)S(1)} collective-permute-done((f32[64,128]{1,0:T(8,128)S(1)}, f32[64,128]{1,0:T(8,128)S(1)}, u32[]{:S(2)}, u32[]{:S(2)}) %collective-permute-start.1) | collective-permute-done | bytes 32800 | tf_op jit(solution)/shard_map/ppermute | solution.py:706
  14.2 0.8 %pack_sums.1 = (f32[32,6,2,128]{3,2,1,0:T(2,128)}, f32[8,128]{1,0:T(8,128)S(1)}) custom-call(f32[6,64,128]{2,1,0:T(8,128)S(1)} %local_sums.1.vec_ref, f32[2,8,128]{2,1,0:T(8,128)S(1)} %get-tuple-element.18.row_ref, f32[64,128]{1,0:T(8,128)S(1)} %collective-permute-done.before_ref, f32[64,128]{1,0:T(8,128)S(1)} %collective-permute-done.1.after_ref, ...), custom_call_target="tpu_custom_call" | custom-call | tf_op jit(solution)/shard_map/pack_sums/pallas_call | solution.py:545
  15.0 9.2 %all-to-all-start = ((f32[32,6,2,128]{3,2,1,0:T(2,128)}), f32[32,6,2,128]{3,2,1,0:T(2,128)S(1)}, u32[]{:S(2)}, u32[]{:S(2)}) async-start(f32[32,6,2,128]{3,2,1,0:T(2,128)} %get-tuple-element.24), calls=%async_computation | async-start | bytes 393216 | tf_op jit(solution)/shard_map/all_to_all | solution.py:710
  24.2 5.1 %slope_solve.1.order.der_in = f32[128,64,128]{2,1,0:T(8,128)} custom-call(f32[8,128]{1,0:T(8,128)S(1)} %copy-done, f32[128]{0:T(128)S(1)} %copy-done.4, f32[128,64,128]{2,1,0:T(8,128)} %v_hbm.5, f32[8,128]{1,0:T(8,128)S(1)} %get-tuple-element.21.order), custom_call_target="tpu_custom_call" | custom-call | flops 12582912 | bytes 12582912 | tf_op jit(solution)/shard_map/slope_solve/pallas_call | solution.py:406
  29.4 3.2 %all-to-all-done.in_ref = f32[32,6,2,128]{3,2,1,0:T(2,128)S(1)} async-done(((f32[32,6,2,128]{3,2,1,0:T(2,128)}), f32[32,6,2,128]{3,2,1,0:T(2,128)S(1)}, u32[]{:S(2)}, u32[]{:S(2)}) %all-to-all-start) | async-done | bytes 196640 | tf_op jit(solution)/shard_map/all_to_all | solution.py:710
  32.5 0.9 %reduced_solve.1 = (f32[32,6,2,128]{3,2,1,0:T(2,128)}, f32[8,128]{1,0:T(8,128)S(1)}) custom-call(f32[3,32,128]{2,1,0:T(8,128)S(1)} %get-tuple-element.23.coef_ref, f32[32,6,2,128]{3,2,1,0:T(2,128)S(1)} %all-to-all-done.in_ref, f32[128,64,128]{2,1,0:T(8,128)} %slope_solve.1.order.der_in), custom_call_target="tpu_custom_call" | custom-call | tf_op jit(solution)/shard_map/reduced_solve/pallas_call | solution.py:597
  33.4 4.2 %all-to-all-start.1 = ((f32[32,6,2,128]{3,2,1,0:T(2,128)}), f32[32,6,2,128]{3,2,1,0:T(2,128)S(1)}, u32[]{:S(2)}, u32[]{:S(2)}) async-start(f32[32,6,2,128]{3,2,1,0:T(2,128)} %get-tuple-element.28), calls=%async_computation.1 | async-start | bytes 393216 | tf_op jit(solution)/shard_map/all_to_all | solution.py:714
  37.6 6.9 %viscous_solve.1 = (f32[32,64,128]{2,1,0:T(8,128)}, f32[96,64,128]{2,1,0:T(8,128)S(1)}) custom-call(f32[128,64,128]{2,1,0:T(8,128)} %v_hbm.5, f32[3,128]{1,0:T(4,128)S(1)} %get-tuple-element.22.line, f32[64,128]{1,0:T(8,128)S(1)} %collective-permute-done.before_ref, f32[64,128]{1,0:T(8,128)S(1)} %collective-permute-done.1.after_ref, f32[1,128]{1,0:T(1,128)S(1)} %bitcast.6, ...), custom_call_target="tpu_custom_call" | custom-call | flops 12582912 | bytes 12582912 | tf_op jit(solution)/shard_map/viscous_solve/pallas_call | solution.py:500
  44.5 1.4 %all-to-all-done.1.edge_ref = f32[32,6,2,128]{3,2,1,0:T(2,128)S(1)} async-done(((f32[32,6,2,128]{3,2,1,0:T(2,128)}), f32[32,6,2,128]{3,2,1,0:T(2,128)S(1)}, u32[]{:S(2)}, u32[]{:S(2)}) %all-to-all-start.1) | async-done | bytes 196640 | tf_op jit(solution)/shard_map/all_to_all | solution.py:714
  46.0 6.0 %final_solve.1 = (f32[128,64,128]{2,1,0:T(8,128)}, f32[128,64,128]{2,1,0:T(8,128)}) custom-call(f32[8,128]{1,0:T(8,128)S(1)} %copy-done, f32[128]{0:T(128)S(1)} %copy-done.4, f32[128,64,128]{2,1,0:T(8,128)} %slope_solve.1.order.der_in, f32[32,64,128]{2,1,0:T(8,128)} %get-tuple-element.26.upd_in, f32[96,64,128]{2,1,0:T(8,128)S(1)} %get-tuple-element.27.kept, ...), custom_call_target="tpu_custom_call" | custom-call | tf_op jit(solution)/shard_map/final_solve/pallas_call | solution.py:679
  (2 shorter events, 0.0 us)
Async XLA Ops:
  0.6 10.5 %copy-start = (f32[8,128]{1,0:T(8,128)S(1)}, f32[8,128]{1,0:T(8,128)}, u32[]{:S(2)}) copy-start(f32[8,128]{1,0:T(8,128)} %constant.2.clone.table) | copy-start | bytes 12292
  0.6 9.6 %copy-start.2 = (f32[4096]{0:T(1024)S(1)}, f32[4096]{0:T(1024)}, u32[]{:S(2)}) copy-start(f32[4096]{0:T(1024)} %param.9) | copy-start | bytes 49156
  0.7 9.6 %copy-start.1 = (f32[4096]{0:T(1024)S(1)}, f32[4096]{0:T(1024)}, u32[]{:S(2)}) copy-start(f32[4096]{0:T(1024)} %param.8) | copy-start | bytes 49156
  0.7 13.5 %copy-start.3 = (f32[128]{0:T(128)S(1)}, f32[128]{0:T(128)}, u32[]{:S(2)}) copy-start(f32[128]{0:T(128)} %param.10) | copy-start | bytes 1540
  0.7 23.5 %copy-start.4 = (f32[128]{0:T(128)S(1)}, f32[128]{0:T(128)}, u32[]{:S(2)}) copy-start(f32[128]{0:T(128)} %metric.3) | copy-start | bytes 1540
  3.5 9.4 %collective-permute-start = (f32[64,128]{1,0:T(8,128)S(1)}, f32[64,128]{1,0:T(8,128)S(1)}, u32[]{:S(2)}, u32[]{:S(2)}) collective-permute-start(f32[64,128]{1,0:T(8,128)S(1)} %get-tuple-element.19), channel_id=1, source_target_pairs={{0,1},{1,2},{2,3},{3,4},{4,5},{5,6},{6,7},{8,9},{9,10},{10,11},{11... | collective-permute-start | bytes 98312 | tf_op jit(solution)/shard_map/ppermute | solution.py:705
  8.3 5.9 %collective-permute-start.1 = (f32[64,128]{1,0:T(8,128)S(1)}, f32[64,128]{1,0:T(8,128)S(1)}, u32[]{:S(2)}, u32[]{:S(2)}) collective-permute-start(f32[64,128]{1,0:T(8,128)S(1)} %get-tuple-element.20), channel_id=1, source_target_pairs={{1,0},{2,1},{3,2},{4,3},{5,4},{6,5},{7,6},{9,8},{10,9},{11,10},{12... | collective-permute-start | bytes 98312 | tf_op jit(solution)/shard_map/ppermute | solution.py:706
  15.0 17.5 %all-to-all-start = ((f32[32,6,2,128]{3,2,1,0:T(2,128)}), f32[32,6,2,128]{3,2,1,0:T(2,128)S(1)}, u32[]{:S(2)}, u32[]{:S(2)}) async-start(f32[32,6,2,128]{3,2,1,0:T(2,128)} %get-tuple-element.24), calls=%async_computation | async-start | bytes 393216 | tf_op jit(solution)/shard_map/all_to_all | solution.py:710
  33.4 12.6 %all-to-all-start.1 = ((f32[32,6,2,128]{3,2,1,0:T(2,128)}), f32[32,6,2,128]{3,2,1,0:T(2,128)S(1)}, u32[]{:S(2)}, u32[]{:S(2)}) async-start(f32[32,6,2,128]{3,2,1,0:T(2,128)} %get-tuple-element.28), calls=%async_computation.1 | async-start | bytes 393216 | tf_op jit(solution)/shard_map/all_to_all | solution.py:714

commit v3 on v2

--- a/solution.py
+++ b/solution.py
@@ -656,14 +656,17 @@
             der[span - 1] = der[span - 1] + (metric[span - 1] * DIRECT) * edges[5]
         row_copy(der, der_hbm, der_to, c, rows).start()
 
-    def near(step, carry):
+    def near_viscous(step, carry):
         viscous_rows(CHUNKS - 1 - step, kept, far * rows)
+        return carry
+
+    def near_slope(step, carry):
         slope_rows(CHUNKS - 1 - step)
         return carry
 
-    viscous_rows(CHUNKS - 1, kept, far * rows)
+    lax.fori_loop(0, KEPT, near_viscous, 0)
     slope_rows(CHUNKS - 1)
-    lax.fori_loop(1, KEPT, near, 0)
+    lax.fori_loop(1, KEPT, near_slope, 0)
     for c in range(far - 1, -1, -1):
         row_copy(upd_in, upd, upd_from, c, rows).wait()
         viscous_rows(c, upd, 0)

time: 52.3 us -> 52.7 us (level)
  no operation moved by 1% of the time
where the time goes in v3:
time: 52.7 us; the launch traced here: 52.4 us
  Pallas kernels  25.7 us (49%)
  starting transfers between devices  20.1 us (38%)
  waiting for transfers between devices  5.81 us (11%)
  between operations  0.78 us (1%)
    all_to_all x1, starting transfers between devices, body(): arrived = lax.all_to_all(packed, 'gx', 0, 0, tiled=True)  9.19 us
    pallas_call x1, Pallas kernels, viscous_solve(): pl.pallas_call(viscous_kernel, out_shape=(pltpu.HBM((span - kept, planes,...  6.91 us
    pallas_call x1, Pallas kernels, final_solve(): pl.pallas_call(final_kernel, out_shape=(result, result), in_specs=in_smem...  6.45 us
    pallas_call x1, Pallas kernels, slope_solve(): pl.pallas_call(slope_kernel, out_shape=pltpu.HBM(velocity.shape, F32), in...  5.14 us
    ppermute x1, starting transfers between devices, body(): before = lax.ppermute(last, 'gy', up)  4.76 us
    all_to_all x1, starting transfers between devices, body(): edge = lax.all_to_all(solved, 'gx', 0, 0, tiled=True)  4.22 us
    all_to_all x1, waiting for transfers between devices, body(): arrived = lax.all_to_all(packed, 'gx', 0, 0, tiled=True)  3.17 us
    pallas_call x1, Pallas kernels, rim_columns(): pl.pallas_call(rim_kernel, out_shape=(pltpu.VMEM(velocity.shape, F32), co...  2.85 us
  transfers between devices with their start and end apart: 4, of which 3 were waited for; matrix products, arithmetic and copies ran while one was open for 0% of the time, Pallas kernels for 28%

profile of v3, /device:TPU:97, one launch (start us, length us, event | category | flops | bytes accessed | tf_op | source)
XLA Modules:
  0.0 52.4 jit_solution(7811006065846079819)
XLA Ops:
  0.6 0.0 copy-start
  0.6 0.0 copy-start.2
  0.7 0.0 copy-start.1
  0.7 0.0 copy-start.3
  0.7 0.0 copy-start.4
  0.7 2.8 %rim_columns.1 = (f32[128,64,128]{2,1,0:T(8,128)S(1)}, f32[64,128]{1,0:T(8,128)S(1)}, f32[64,128]{1,0:T(8,128)S(1)}) custom-call(f32[128,64,128]{2,1,0:T(8,128)} %v_hbm.5), custom_call_target="tpu_custom_call" | custom-call | tf_op jit(solution)/shard_map/rim_columns/pallas_call | solution.py:299
  3.5 4.8 %collective-permute-start = (f32[64,128]{1,0:T(8,128)S(1)}, f32[64,128]{1,0:T(8,128)S(1)}, u32[]{:S(2)}, u32[]{:S(2)}) collective-permute-start(f32[64,128]{1,0:T(8,128)S(1)} %get-tuple-element.19), channel_id=1, source_target_pairs={{0,1},{1,2},{2,3},{3,4},{4,5},{5,6},{6,7},{8,9},{9,10},{10,11},{11... | collective-permute-start | bytes 98312 | tf_op jit(solution)/shard_map/ppermute | solution.py:708
  8.3 1.9 %collective-permute-start.1 = (f32[64,128]{1,0:T(8,128)S(1)}, f32[64,128]{1,0:T(8,128)S(1)}, u32[]{:S(2)}, u32[]{:S(2)}) collective-permute-start(f32[64,128]{1,0:T(8,128)S(1)} %get-tuple-element.20), channel_id=1, source_target_pairs={{1,0},{2,1},{3,2},{4,3},{5,4},{6,5},{7,6},{9,8},{10,9},{11,10},{12... | collective-permute-start | bytes 98312 | tf_op jit(solution)/shard_map/ppermute | solution.py:709
  10.2 0.0 copy-done.2
  10.2 0.9 %block_terms.1 = (f32[3,128]{1,0:T(4,128)S(1)}, f32[2,128,128]{2,1,0:T(8,128)S(1)}, f32[2,128]{1,0:T(2,128)S(1)}, f32[2,8,128]{2,1,0:T(8,128)S(1)}, f32[3,32,128]{2,1,0:T(8,128)S(1)}) custom-call(f32[32,128]{1,0:T(8,128)S(1)} %bitcast.3, f32[32,128]{1,0:T(8,128)S(1)} %bitcast.4), custom_call_target="tpu_custom_call" | custom-call | flops 4194304 | bytes 1048576 | tf_op jit(solution)/shard_map/block_terms/pallas_call | solution.py:255
  11.1 0.0 copy-done
  11.1 1.8 %local_sums.1.vec_ref = f32[6,64,128]{2,1,0:T(8,128)S(1)} custom-call(f32[8,128]{1,0:T(8,128)S(1)} %copy-done, f32[128,64,128]{2,1,0:T(8,128)S(1)} %get-tuple-element.16.v_ref, f32[2,128,128]{2,1,0:T(8,128)S(1)} %get-tuple-element.17.weight), custom_call_target="tpu_custom_call" | custom-call | flops 8388608 | bytes 4194304 | tf_op jit(solution)/shard_map/local_sums/pallas_call | solution.py:335
  12.9 0.0 collective-permute-done.before_ref
  12.9 1.2 %collective-permute-done.1.after_ref = f32[64,128]{1,0:T(8,128)S(1)} collective-permute-done((f32[64,128]{1,0:T(8,128)S(1)}, f32[64,128]{1,0:T(8,128)S(1)}, u32[]{:S(2)}, u32[]{:S(2)}) %collective-permute-start.1) | collective-permute-done | bytes 32800 | tf_op jit(solution)/shard_map/ppermute | solution.py:709
  14.2 0.8 %pack_sums.1 = (f32[32,6,2,128]{3,2,1,0:T(2,128)}, f32[8,128]{1,0:T(8,128)S(1)}) custom-call(f32[6,64,128]{2,1,0:T(8,128)S(1)} %local_sums.1.vec_ref, f32[2,8,128]{2,1,0:T(8,128)S(1)} %get-tuple-element.18.row_ref, f32[64,128]{1,0:T(8,128)S(1)} %collective-permute-done.before_ref, f32[64,128]{1,0:T(8,128)S(1)} %collective-permute-done.1.after_ref, ...), custom_call_target="tpu_custom_call" | custom-call | tf_op jit(solution)/shard_map/pack_sums/pallas_call | solution.py:545
  15.0 9.2 %all-to-all-start = ((f32[32,6,2,128]{3,2,1,0:T(2,128)}), f32[32,6,2,128]{3,2,1,0:T(2,128)S(1)}, u32[]{:S(2)}, u32[]{:S(2)}) async-start(f32[32,6,2,128]{3,2,1,0:T(2,128)} %get-tuple-element.24), calls=%async_computation | async-start | bytes 393216 | tf_op jit(solution)/shard_map/all_to_all | solution.py:713
  24.2 0.0 copy-done.4
  24.2 5.1 %slope_solve.1.order.der_in = f32[128,64,128]{2,1,0:T(8,128)} custom-call(f32[8,128]{1,0:T(8,128)S(1)} %copy-done, f32[128]{0:T(128)S(1)} %copy-done.4, f32[128,64,128]{2,1,0:T(8,128)} %v_hbm.5, f32[8,128]{1,0:T(8,128)S(1)} %get-tuple-element.21.order), custom_call_target="tpu_custom_call" | custom-call | flops 12582912 | bytes 12582912 | tf_op jit(solution)/shard_map/slope_solve/pallas_call | solution.py:406
  29.4 3.2 %all-to-all-done.in_ref = f32[32,6,2,128]{3,2,1,0:T(2,128)S(1)} async-done(((f32[32,6,2,128]{3,2,1,0:T(2,128)}), f32[32,6,2,128]{3,2,1,0:T(2,128)S(1)}, u32[]{:S(2)}, u32[]{:S(2)}) %all-to-all-start) | async-done | bytes 196640 | tf_op jit(solution)/shard_map/all_to_all | solution.py:713
  32.5 0.9 %reduced_solve.1 = (f32[32,6,2,128]{3,2,1,0:T(2,128)}, f32[8,128]{1,0:T(8,128)S(1)}) custom-call(f32[3,32,128]{2,1,0:T(8,128)S(1)} %get-tuple-element.23.coef_ref, f32[32,6,2,128]{3,2,1,0:T(2,128)S(1)} %all-to-all-done.in_ref, f32[128,64,128]{2,1,0:T(8,128)} %slope_solve.1.order.der_in), custom_call_target="tpu_custom_call" | custom-call | tf_op jit(solution)/shard_map/reduced_solve/pallas_call | solution.py:597
  33.4 4.2 %all-to-all-start.1 = ((f32[32,6,2,128]{3,2,1,0:T(2,128)}), f32[32,6,2,128]{3,2,1,0:T(2,128)S(1)}, u32[]{:S(2)}, u32[]{:S(2)}) async-start(f32[32,6,2,128]{3,2,1,0:T(2,128)} %get-tuple-element.28), calls=%async_computation.1 | async-start | bytes 393216 | tf_op jit(solution)/shard_map/all_to_all | solution.py:717
  37.6 6.9 %viscous_solve.1 = (f32[32,64,128]{2,1,0:T(8,128)}, f32[96,64,128]{2,1,0:T(8,128)S(1)}) custom-call(f32[128,64,128]{2,1,0:T(8,128)} %v_hbm.5, f32[3,128]{1,0:T(4,128)S(1)} %get-tuple-element.22.line, f32[64,128]{1,0:T(8,128)S(1)} %collective-permute-done.before_ref, f32[64,128]{1,0:T(8,128)S(1)} %collective-permute-done.1.after_ref, f32[1,128]{1,0:T(1,128)S(1)} %bitcast.6, ...), custom_call_target="tpu_custom_call" | custom-call | flops 12582912 | bytes 12582912 | tf_op jit(solution)/shard_map/viscous_solve/pallas_call | solution.py:500
  44.5 1.4 %all-to-all-done.1.edge_ref = f32[32,6,2,128]{3,2,1,0:T(2,128)S(1)} async-done(((f32[32,6,2,128]{3,2,1,0:T(2,128)}), f32[32,6,2,128]{3,2,1,0:T(2,128)S(1)}, u32[]{:S(2)}, u32[]{:S(2)}) %all-to-all-start.1) | async-done | bytes 196640 | tf_op jit(solution)/shard_map/all_to_all | solution.py:717
  46.0 6.5 %final_solve.1 = (f32[128,64,128]{2,1,0:T(8,128)}, f32[128,64,128]{2,1,0:T(8,128)}) custom-call(f32[8,128]{1,0:T(8,128)S(1)} %copy-done, f32[128]{0:T(128)S(1)} %copy-done.4, f32[128,64,128]{2,1,0:T(8,128)} %slope_solve.1.order.der_in, f32[32,64,128]{2,1,0:T(8,128)} %get-tuple-element.26.upd_in, f32[96,64,128]{2,1,0:T(8,128)S(1)} %get-tuple-element.27.kept, ...), custom_call_target="tpu_custom_call" | custom-call | tf_op jit(solution)/shard_map/final_solve/pallas_call | solution.py:682
  (2 shorter events, 0.0 us)
Async XLA Ops:
  0.6 10.5 %copy-start = (f32[8,128]{1,0:T(8,128)S(1)}, f32[8,128]{1,0:T(8,128)}, u32[]{:S(2)}) copy-start(f32[8,128]{1,0:T(8,128)} %constant.2.clone.table) | copy-start | bytes 12292
  0.6 9.6 %copy-start.2 = (f32[4096]{0:T(1024)S(1)}, f32[4096]{0:T(1024)}, u32[]{:S(2)}) copy-start(f32[4096]{0:T(1024)} %param.9) | copy-start | bytes 49156
  0.7 9.6 %copy-start.1 = (f32[4096]{0:T(1024)S(1)}, f32[4096]{0:T(1024)}, u32[]{:S(2)}) copy-start(f32[4096]{0:T(1024)} %param.8) | copy-start | bytes 49156
  0.7 13.5 %copy-start.3 = (f32[128]{0:T(128)S(1)}, f32[128]{0:T(128)}, u32[]{:S(2)}) copy-start(f32[128]{0:T(128)} %param.10) | copy-start | bytes 1540
  0.7 23.5 %copy-start.4 = (f32[128]{0:T(128)S(1)}, f32[128]{0:T(128)}, u32[]{:S(2)}) copy-start(f32[128]{0:T(128)} %metric.3) | copy-start | bytes 1540
  3.5 9.4 %collective-permute-start = (f32[64,128]{1,0:T(8,128)S(1)}, f32[64,128]{1,0:T(8,128)S(1)}, u32[]{:S(2)}, u32[]{:S(2)}) collective-permute-start(f32[64,128]{1,0:T(8,128)S(1)} %get-tuple-element.19), channel_id=1, source_target_pairs={{0,1},{1,2},{2,3},{3,4},{4,5},{5,6},{6,7},{8,9},{9,10},{10,11},{11... | collective-permute-start | bytes 98312 | tf_op jit(solution)/shard_map/ppermute | solution.py:708
  8.3 5.9 %collective-permute-start.1 = (f32[64,128]{1,0:T(8,128)S(1)}, f32[64,128]{1,0:T(8,128)S(1)}, u32[]{:S(2)}, u32[]{:S(2)}) collective-permute-start(f32[64,128]{1,0:T(8,128)S(1)} %get-tuple-element.20), channel_id=1, source_target_pairs={{1,0},{2,1},{3,2},{4,3},{5,4},{6,5},{7,6},{9,8},{10,9},{11,10},{12... | collective-permute-start | bytes 98312 | tf_op jit(solution)/shard_map/ppermute | solution.py:709
  15.0 17.5 %all-to-all-start = ((f32[32,6,2,128]{3,2,1,0:T(2,128)}), f32[32,6,2,128]{3,2,1,0:T(2,128)S(1)}, u32[]{:S(2)}, u32[]{:S(2)}) async-start(f32[32,6,2,128]{3,2,1,0:T(2,128)} %get-tuple-element.24), calls=%async_computation | async-start | bytes 393216 | tf_op jit(solution)/shard_map/all_to_all | solution.py:713
  33.4 12.6 %all-to-all-start.1 = ((f32[32,6,2,128]{3,2,1,0:T(2,128)}), f32[32,6,2,128]{3,2,1,0:T(2,128)S(1)}, u32[]{:S(2)}, u32[]{:S(2)}) async-start(f32[32,6,2,128]{3,2,1,0:T(2,128)} %get-tuple-element.28), calls=%async_computation.1 | async-start | bytes 393216 | tf_op jit(solution)/shard_map/all_to_all | solution.py:717
